TPU v7x, 32 devices: a whole 2x2x4 slice. The times are simulated.
32 devices in a mesh: fsdp: 32 (over z, y, x, core).
Axes of the slice: x: 2, y: 2, z: 4, core: 2. Of those that a mesh axis runs over, the one named last changes fastest.
Arguments:
- tokens: bfloat16 [32768, 768], P('fsdp'), may hold values from -6 to 6
- lengths: int32 [64], P('fsdp'), may hold values from 1 to 512, as said below
- query_weight: bfloat16 [768, 768], P('fsdp'), may hold values from -0.4375 to 0.4375
- key_weight: bfloat16 [768, 768], P('fsdp'), may hold values from -0.21875 to 0.21875
- value_weight: bfloat16 [768, 768], P('fsdp'), may hold values from -0.21875 to 0.21875
- out_weight: bfloat16 [768, 768], P('fsdp'), may hold values from -0.875 to 0.875
- query_bias: bfloat16 [768], P('fsdp'), may hold values from -3 to 3
- value_bias: bfloat16 [768], P('fsdp'), may hold values from -3 to 3
- out_bias: bfloat16 [768], P('fsdp'), may hold values from -3 to 3
- first_gain: bfloat16 [768], P('fsdp'), may hold values from 0.099609375 to 1.8984375
- first_shift: bfloat16 [768], P('fsdp'), may hold values from -3 to 3
- up_weight: bfloat16 [768, 3072], P('fsdp'), may hold values from -0.21875 to 0.21875
- down_weight: bfloat16 [3072, 768], P('fsdp'), may hold values from -0.21875 to 0.21875
- up_bias: bfloat16 [3072], P('fsdp'), may hold values from -3 to 3
- down_bias: bfloat16 [768], P('fsdp'), may hold values from -3 to 3
- second_gain: bfloat16 [768], P('fsdp'), may hold values from 0.099609375 to 1.8984375
- second_shift: bfloat16 [768], P('fsdp'), may hold values from -3 to 3
- cotangent: bfloat16 [32768, 768], P('fsdp'), may hold values from -6 to 6
Outputs:
- layer_out: bfloat16 [32768, 768], P('fsdp')
- token_grad: bfloat16 [32768, 768], P('fsdp')
- query_weight_grad: float32 [768, 768], P('fsdp')
- key_weight_grad: float32 [768, 768], P('fsdp')
- value_weight_grad: float32 [768, 768], P('fsdp')
- out_weight_grad: float32 [768, 768], P('fsdp')
- query_bias_grad: float32 [768], P('fsdp')
- value_bias_grad: float32 [768], P('fsdp')
- out_bias_grad: float32 [768], P('fsdp')
- first_gain_grad: float32 [768], P('fsdp')
- first_shift_grad: float32 [768], P('fsdp')
- up_weight_grad: float32 [768, 3072], P('fsdp')
- down_weight_grad: float32 [3072, 768], P('fsdp')
- up_bias_grad: float32 [3072], P('fsdp')
- down_bias_grad: float32 [768], P('fsdp')
- second_gain_grad: float32 [768], P('fsdp')
- second_shift_grad: float32 [768], P('fsdp')
Inputs may be any that keep to these rules, and one draw needn't show every extreme that they name: `lengths`: some sequence has exactly 512 valid positions and some exactly 1.
All inputs are finite; a program needn't handle non-finite values.
Results may differ from a plain program's by a relative error of at most 0.015.
The roundings to bfloat16 on the way count: a program that leaves them out, or rounds other values in their place, can miss the bound.
Values may be sent and summed in bfloat16 or wider, within the bound.
A program may use at most 192 MiB of HBM per device.

v0:
```python
import math

import jax
import jax.numpy as jnp
from jax import lax
from jax.sharding import PartitionSpec as P

HEAD_DIM = 64
MICRO = 2


NEGATIVE = -1e30
EPSILON = 1e-06


def layer_norm(hidden, gain_vector, offset):
    center = hidden - jnp.mean(hidden, axis=-1, keepdims=True)
    spread = jnp.mean(center * center, axis=-1, keepdims=True)
    return center * lax.rsqrt(spread + EPSILON) * gain_vector + offset


def gelu_exact(upward):
    return jax.nn.gelu(upward, approximate=False)


def times_plain(left_side, right_side):
    return jnp.dot(left_side, right_side, preferred_element_type=jnp.float32)


def times_across(left_side, right_side):
    return lax.dot_general(
        left_side, right_side, (((0,), (0,)), ((), ())), preferred_element_type=jnp.float32
    )


def times_back(left_side, right_side):
    return lax.dot_general(
        left_side, right_side, (((1,), (1,)), ((), ())), preferred_element_type=jnp.float32
    )


def column_sum(matrix):
    return jnp.sum(matrix.astype(jnp.float32), axis=0)


def split_heads(matrix, slot_count):
    row_count, model_width = matrix.shape
    return matrix.reshape(slot_count, row_count // slot_count, model_width // HEAD_DIM, HEAD_DIM)


def merge_heads(tensor):
    return tensor.reshape(tensor.shape[0] * tensor.shape[1], tensor.shape[2] * tensor.shape[3])


def attention_scores(queries, key_vectors, key_valid):
    scores = jnp.einsum("sqhd,skhd->shqk", queries, key_vectors, preferred_element_type=jnp.float32)
    scores = scores * (1.0 / math.sqrt(HEAD_DIM))
    return jnp.where(key_valid[:, None, None, :], scores, NEGATIVE)


def forward_pass(tokens_micro, lengths_micro, attention_full, feed_full):
    (
        query_weight,
        key_weight,
        value_weight,
        out_weight,
        query_bias,
        value_bias,
        out_bias,
        first_gain,
        first_shift,
    ) = attention_full
    up_weight, down_weight, up_bias, down_bias, second_gain, second_shift = feed_full
    slot_count = lengths_micro.shape[0]
    seq_length = tokens_micro.shape[0] // slot_count
    positions = lax.broadcasted_iota(jnp.int32, (slot_count, seq_length), 1)
    key_valid = positions < lengths_micro[:, None]
    queries = (times_plain(tokens_micro, query_weight) + query_bias.astype(jnp.float32)).astype(
        jnp.bfloat16
    )
    key_vectors = times_plain(tokens_micro, key_weight).astype(jnp.bfloat16)
    values = (times_plain(tokens_micro, value_weight) + value_bias.astype(jnp.float32)).astype(
        jnp.bfloat16
    )
    query_heads = split_heads(queries, slot_count)
    value_heads = split_heads(values, slot_count)
    scores = attention_scores(query_heads, split_heads(key_vectors, slot_count), key_valid)
    highest_score = jnp.max(scores, axis=-1, keepdims=True)
    raised = jnp.exp(scores - highest_score)
    totals = jnp.sum(raised, axis=-1, keepdims=True)
    probs = (raised / totals).astype(jnp.bfloat16)
    log_total = highest_score + jnp.log(totals)
    context = jnp.einsum("shqk,skhd->sqhd", probs, value_heads, preferred_element_type=jnp.float32)
    context = merge_heads(context).astype(jnp.bfloat16)
    branch = times_plain(context, out_weight) + out_bias.astype(jnp.float32)
    first_sum = tokens_micro.astype(jnp.float32) + branch
    normed = layer_norm(first_sum, first_gain.astype(jnp.float32), first_shift.astype(jnp.float32))
    normed_low = normed.astype(jnp.bfloat16)
    upward = times_plain(normed_low, up_weight) + up_bias.astype(jnp.float32)
    activated = gelu_exact(upward).astype(jnp.bfloat16)
    second_sum = normed + (times_plain(activated, down_weight) + down_bias.astype(jnp.float32))
    output = layer_norm(
        second_sum, second_gain.astype(jnp.float32), second_shift.astype(jnp.float32)
    )
    stored = (
        tokens_micro,
        key_valid,
        queries,
        key_vectors,
        values,
        log_total,
        context,
        first_sum,
        normed_low,
        upward,
        activated,
        second_sum,
    )
    return (output.astype(jnp.bfloat16), stored)


def backward_pass(stored, cotangent_micro, attention_full, feed_full):
    (
        query_weight,
        key_weight,
        value_weight,
        out_weight,
        query_bias,
        value_bias,
        out_bias,
        first_gain,
        first_shift,
    ) = attention_full
    up_weight, down_weight, up_bias, down_bias, second_gain, second_shift = feed_full
    (
        tokens_micro,
        key_valid,
        queries,
        key_vectors,
        values,
        log_total,
        context,
        first_sum,
        normed_low,
        upward,
        activated,
        second_sum,
    ) = stored
    slot_count = key_valid.shape[0]
    row_valid = key_valid.reshape(-1, 1).astype(jnp.float32)
    grad_output = cotangent_micro.astype(jnp.float32) * row_valid
    _, pull_second = jax.vjp(
        layer_norm, second_sum, second_gain.astype(jnp.float32), second_shift.astype(jnp.float32)
    )
    grad_second, second_gain_term, second_shift_term = pull_second(grad_output)
    grad_feed = grad_second.astype(jnp.bfloat16)
    down_weight_term = times_across(activated, grad_feed)
    down_bias_term = column_sum(grad_feed)
    grad_activated = times_back(grad_feed, down_weight)
    _, pull_gelu = jax.vjp(gelu_exact, upward)
    grad_up = pull_gelu(grad_activated)[0].astype(jnp.bfloat16)
    up_weight_term = times_across(normed_low, grad_up)
    up_bias_term = column_sum(grad_up)
    grad_normed = grad_second + times_back(grad_up, up_weight)
    _, pull_first = jax.vjp(
        layer_norm, first_sum, first_gain.astype(jnp.float32), first_shift.astype(jnp.float32)
    )
    grad_first, first_gain_term, first_shift_term = pull_first(grad_normed)
    grad_branch = grad_first.astype(jnp.bfloat16)
    out_weight_term = times_across(context, grad_branch)
    out_bias_term = column_sum(grad_branch)
    grad_context = split_heads(times_back(grad_branch, out_weight).astype(jnp.bfloat16), slot_count)
    query_heads = split_heads(queries, slot_count)
    key_heads = split_heads(key_vectors, slot_count)
    value_heads = split_heads(values, slot_count)
    probs = jnp.exp(attention_scores(query_heads, key_heads, key_valid) - log_total)
    grad_probs = jnp.einsum(
        "sqhd,skhd->shqk", grad_context, value_heads, preferred_element_type=jnp.float32
    )
    grad_values = jnp.einsum(
        "shqk,sqhd->skhd",
        probs.astype(jnp.bfloat16),
        grad_context,
        preferred_element_type=jnp.float32,
    )
    grad_values = merge_heads(grad_values).astype(jnp.bfloat16)
    row_delta = jnp.sum(grad_probs * probs, axis=-1, keepdims=True)
    grad_scores = (probs * (grad_probs - row_delta)).astype(jnp.bfloat16)
    score_scale = 1.0 / math.sqrt(HEAD_DIM)
    grad_queries = jnp.einsum(
        "shqk,skhd->sqhd", grad_scores, key_heads, preferred_element_type=jnp.float32
    )
    grad_queries = (merge_heads(grad_queries) * score_scale).astype(jnp.bfloat16)
    grad_keys = jnp.einsum(
        "shqk,sqhd->skhd", grad_scores, query_heads, preferred_element_type=jnp.float32
    )
    grad_keys = (merge_heads(grad_keys) * score_scale).astype(jnp.bfloat16)
    query_weight_term = times_across(tokens_micro, grad_queries)
    key_weight_term = times_across(tokens_micro, grad_keys)
    value_weight_term = times_across(tokens_micro, grad_values)
    input_grad = (
        grad_first
        + times_back(grad_queries, query_weight)
        + times_back(grad_keys, key_weight)
        + times_back(grad_values, value_weight)
    ).astype(jnp.bfloat16)
    attention_terms = (
        query_weight_term,
        key_weight_term,
        value_weight_term,
        out_weight_term,
        column_sum(grad_queries),
        column_sum(grad_values),
        out_bias_term,
        first_gain_term,
        first_shift_term,
    )
    feed_terms = (
        up_weight_term,
        down_weight_term,
        up_bias_term,
        down_bias_term,
        second_gain_term,
        second_shift_term,
    )
    return (input_grad, attention_terms, feed_terms)


def add_terms(running, fresh):
    if running is None:
        return fresh
    return tuple((left_side + right_side for left_side, right_side in zip(running, fresh)))


def shards(
    tokens,
    lengths,
    query_weight,
    key_weight,
    value_weight,
    out_weight,
    query_bias,
    value_bias,
    out_bias,
    first_gain,
    first_shift,
    up_weight,
    down_weight,
    up_bias,
    down_bias,
    second_gain,
    second_shift,
    cotangent,
):

    def fetch_backward():
        feed_full = (
            lax.all_gather(up_weight, "fsdp", axis=0, tiled=True),
            lax.all_gather(down_weight, "fsdp", axis=0, tiled=True),
            lax.all_gather(up_bias, "fsdp", axis=0, tiled=True),
            lax.all_gather(down_bias, "fsdp", axis=0, tiled=True),
            lax.all_gather(second_gain, "fsdp", axis=0, tiled=True),
            lax.all_gather(second_shift, "fsdp", axis=0, tiled=True),
        )
        attention_full = (
            lax.all_gather(query_weight, "fsdp", axis=0, tiled=True),
            lax.all_gather(key_weight, "fsdp", axis=0, tiled=True),
            lax.all_gather(value_weight, "fsdp", axis=0, tiled=True),
            lax.all_gather(out_weight, "fsdp", axis=0, tiled=True),
            lax.all_gather(query_bias, "fsdp", axis=0, tiled=True),
            lax.all_gather(value_bias, "fsdp", axis=0, tiled=True),
            lax.all_gather(out_bias, "fsdp", axis=0, tiled=True),
            lax.all_gather(first_gain, "fsdp", axis=0, tiled=True),
            lax.all_gather(first_shift, "fsdp", axis=0, tiled=True),
        )
        return (attention_full, feed_full)

    micro_count = MICRO
    micro_rows = tokens.shape[0] // micro_count
    micro_slots = lengths.shape[0] // micro_count
    outputs = []
    stored_list = []
    for micro_index in range(micro_count):
        fetch_attention_full = (
            lax.all_gather(query_weight, "fsdp", axis=0, tiled=True),
            lax.all_gather(key_weight, "fsdp", axis=0, tiled=True),
            lax.all_gather(value_weight, "fsdp", axis=0, tiled=True),
            lax.all_gather(out_weight, "fsdp", axis=0, tiled=True),
            lax.all_gather(query_bias, "fsdp", axis=0, tiled=True),
            lax.all_gather(value_bias, "fsdp", axis=0, tiled=True),
            lax.all_gather(out_bias, "fsdp", axis=0, tiled=True),
            lax.all_gather(first_gain, "fsdp", axis=0, tiled=True),
            lax.all_gather(first_shift, "fsdp", axis=0, tiled=True),
        )
        fetch_feed_full = (
            lax.all_gather(up_weight, "fsdp", axis=0, tiled=True),
            lax.all_gather(down_weight, "fsdp", axis=0, tiled=True),
            lax.all_gather(up_bias, "fsdp", axis=0, tiled=True),
            lax.all_gather(down_bias, "fsdp", axis=0, tiled=True),
            lax.all_gather(second_gain, "fsdp", axis=0, tiled=True),
            lax.all_gather(second_shift, "fsdp", axis=0, tiled=True),
        )
        attention_full = fetch_attention_full
        feed_full = fetch_feed_full
        row_start = micro_index * micro_rows
        slot_start = micro_index * micro_slots
        output, stored = forward_pass(
            tokens[row_start : row_start + micro_rows],
            lengths[slot_start : slot_start + micro_slots],
            attention_full,
            feed_full,
        )
        outputs.append(output)
        stored_list.append(stored)
    input_grads = [None] * micro_count
    attention_total = None
    feed_total = None
    attention_owned = None
    feed_owned = None
    for micro_index in reversed(range(micro_count)):
        attention_full, feed_full = fetch_backward()
        row_start = micro_index * micro_rows
        input_grad, attention_terms, feed_terms = backward_pass(
            stored_list[micro_index],
            cotangent[row_start : row_start + micro_rows],
            attention_full,
            feed_full,
        )
        input_grads[micro_index] = input_grad
        attention_total = add_terms(attention_total, attention_terms)
        feed_total = add_terms(feed_total, feed_terms)
    (
        query_weight_sum,
        key_weight_sum,
        value_weight_sum,
        out_weight_sum,
        query_bias_sum,
        value_bias_sum,
        out_bias_sum,
        first_gain_sum,
        first_shift_sum,
    ) = attention_total
    (
        up_weight_sum,
        down_weight_sum,
        up_bias_sum,
        down_bias_sum,
        second_gain_sum,
        second_shift_sum,
    ) = feed_total
    attention_owned = (
        lax.psum_scatter(query_weight_sum, "fsdp", scatter_dimension=0, tiled=True),
        lax.psum_scatter(key_weight_sum, "fsdp", scatter_dimension=0, tiled=True),
        lax.psum_scatter(value_weight_sum, "fsdp", scatter_dimension=0, tiled=True),
        lax.psum_scatter(out_weight_sum, "fsdp", scatter_dimension=0, tiled=True),
        lax.psum_scatter(query_bias_sum, "fsdp", scatter_dimension=0, tiled=True),
        lax.psum_scatter(value_bias_sum, "fsdp", scatter_dimension=0, tiled=True),
        lax.psum_scatter(out_bias_sum, "fsdp", scatter_dimension=0, tiled=True),
        lax.psum_scatter(first_gain_sum, "fsdp", scatter_dimension=0, tiled=True),
        lax.psum_scatter(first_shift_sum, "fsdp", scatter_dimension=0, tiled=True),
    )
    feed_owned = (
        lax.psum_scatter(up_weight_sum, "fsdp", scatter_dimension=0, tiled=True),
        lax.psum_scatter(down_weight_sum, "fsdp", scatter_dimension=0, tiled=True),
        lax.psum_scatter(up_bias_sum, "fsdp", scatter_dimension=0, tiled=True),
        lax.psum_scatter(down_bias_sum, "fsdp", scatter_dimension=0, tiled=True),
        lax.psum_scatter(second_gain_sum, "fsdp", scatter_dimension=0, tiled=True),
        lax.psum_scatter(second_shift_sum, "fsdp", scatter_dimension=0, tiled=True),
    )
    return (
        jnp.concatenate(outputs, axis=0),
        jnp.concatenate(input_grads, axis=0),
        attention_owned[0],
        attention_owned[1],
        attention_owned[2],
        attention_owned[3],
        attention_owned[4],
        attention_owned[5],
        attention_owned[6],
        attention_owned[7],
        attention_owned[8],
        feed_owned[0],
        feed_owned[1],
        feed_owned[2],
        feed_owned[3],
        feed_owned[4],
        feed_owned[5],
    )


def solution(mesh):
    return jax.shard_map(
        shards,
        mesh=mesh,
        in_specs=(
            P("fsdp", None),
            P("fsdp"),
            P("fsdp", None),
            P("fsdp", None),
            P("fsdp", None),
            P("fsdp", None),
            P("fsdp"),
            P("fsdp"),
            P("fsdp"),
            P("fsdp"),
            P("fsdp"),
            P("fsdp", None),
            P("fsdp", None),
            P("fsdp"),
            P("fsdp"),
            P("fsdp"),
            P("fsdp"),
            P("fsdp", None),
        ),
        out_specs=(
            P("fsdp", None),
            P("fsdp", None),
            P("fsdp", None),
            P("fsdp", None),
            P("fsdp", None),
            P("fsdp", None),
            P("fsdp"),
            P("fsdp"),
            P("fsdp"),
            P("fsdp"),
            P("fsdp"),
            P("fsdp", None),
            P("fsdp", None),
            P("fsdp"),
            P("fsdp"),
            P("fsdp"),
            P("fsdp"),
        ),
        check_vma=False,
    )
```

profile of v0, /device:TPU:0, one launch (start us, length us, event | category | flops | bytes accessed | tf_op | source)
XLA Modules:
  0.0 1137.6 jit_solution(5422746597143475728)
XLA Ops:
  23.8 42.6 %all-reduce.19 = (bf16[768]{0:T(1024)(128)(2,1)S(1)}, bf16[768]{0:T(1024)(128)(2,1)S(1)}, bf16[768]{0:T(1024)(128)(2,1)S(1)}, bf16[768]{0:T(1024)(128)(2,1)S(1)}...) all-reduce(bf16[768]{0:T(1024)(128)(2,1)S(1)} %dynamic-update-slice, ...), channel_id=1, replica_groups=mesh['fsdp'=32] {'fsdp'}, use_global_device_ids=true, to_apply=%add | all-reduce | flops 9216 | bytes 36864
  70.4 53.2 %all-gather.11.cloned.1.call-done = bf16[768,768]{1,0:T(8,128)(2,1)} async-done(((bf16[24,768]{1,0:T(8,128)(2,1)}), bf16[768,768]{1,0:T(8,128)(2,1)}) %all-gather.11.cloned.1.call-update) | async-done | bytes 1179664 | tf_op jit(solution)/shard_map/all_gather | solution.py:286
  128.0 51.6 %all-gather.7.cloned.1.call-done = bf16[768,768]{1,0:T(8,128)(2,1)} async-done(((bf16[24,768]{1,0:T(8,128)(2,1)}), bf16[768,768]{1,0:T(8,128)(2,1)}) %all-gather.7.cloned.1.call-update) | async-done | bytes 1179664 | tf_op jit(solution)/shard_map/all_gather | solution.py:287
  196.1 39.3 %all-gather.13.cloned.1.call-done = bf16[768,768]{1,0:T(8,128)(2,1)} async-done(((bf16[24,768]{1,0:T(8,128)(2,1)}), bf16[768,768]{1,0:T(8,128)(2,1)}) %all-gather.13.cloned.1.call-update) | async-done | bytes 1179664 | tf_op jit(solution)/shard_map/all_gather | solution.py:288
  253.2 4.1 fusion.75
  267.9 32.7 %all-gather.15.cloned.1.call-done = bf16[768,3072]{1,0:T(8,128)(2,1)} async-done(((bf16[24,3072]{1,0:T(8,128)(2,1)}), bf16[768,3072]{1,0:T(8,128)(2,1)}) %all-gather.15.cloned.1.call-update) | async-done | bytes 4718608 | tf_op jit(solution)/shard_map/all_gather | solution.py:296
  300.6 5.3 fusion.61
  308.5 34.9 %multiply_convert_fusion.3 = (bf16[512,3072]{1,0:T(8,128)(2,1)}, f32[512,3072]{1,0:T(8,128)}, bf16[512,3072]{1,0:T(8,128)(2,1)}, f32[512,3072]{1,0:T(8,128)}, f32[512,3072]{1,0:T(8,128)}) fusion(f32[3072]{0:T(1024)S(1)} %convert_element_type.321, f32[512,3072]{1,0:T(8,128)S(1)} %fusion.61, bf16[768,3072]{1,0:T(8,128)(2,1)S(1)} %copy-done.59, ...), kind=kOutput, calls=%fused_computation.41 | convolution fusion | flops 2625503232 | bytes 37771264 | tf_op jit(solution)/shard_map/dot_general | solution.py:27
  343.5 22.4 %all-gather.17.cloned.1.call-done = bf16[3072,768]{1,0:T(8,128)(2,1)} async-done(((bf16[96,768]{1,0:T(8,128)(2,1)}), bf16[3072,768]{1,0:T(8,128)(2,1)}) %all-gather.17.cloned.1.call-update) | async-done | bytes 4718608 | tf_op jit(solution)/shard_map/all_gather | solution.py:297
  365.9 6.2 fusion.78
  382.4 4.8 fusion.81
  387.2 17.6 %convert_reduce_fusion = (f32[3072]{0:T(1024)S(1)}, bf16[512,3072]{1,0:T(8,128)(2,1)}, f32[3072]{0:T(1024)S(1)}, bf16[512,3072]{1,0:T(8,128)(2,1)}) fusion(f32[512,3072]{1,0:T(8,128)} %get-tuple-element.121, f32[512,3072]{1,0:T(8,128)} %get-tuple-element.148, f32[3072]{0:T(1024)S(1)} %convert_element_type.321, f32[512,3072]{1,0:T(8,128)} %fusion.81, ...), kind=kOutput, calls=%fused_computation.22 | convolution fusion | flops 2469390336 | bytes 43290624 | tf_op jit(solution)/shard_map/dot_general | solution.py:37
  404.8 6.1 add_add_fusion.8
  410.9 5.8 multiply_reduce_fusion.4
  437.1 6.8 convert_reduce_fusion.6
  444.0 7.2 convert_reduce_fusion.7
  458.3 8.1 multiply_reduce_fusion
  466.4 7.1 multiply_convert_fusion
  481.3 10.7 multiply_reduce_fusion.1
  492.9 7.0 multiply_convert_fusion.1
  509.1 4.2 convert_reduce_fusion.9
  515.0 4.0 convert_reduce_fusion.8
  526.4 4.8 fusion.85
  531.2 5.3 convolution_add_fusion
  538.0 5.0 fusion.59
  542.9 5.8 convolution_add_fusion.1
  549.0 41.0 %all-reduce.18 = (f32[768]{0:T(1024)S(1)}, f32[768]{0:T(1024)S(1)}, f32[768]{0:T(1024)S(1)}, f32[768]{0:T(1024)S(1)}, f32[768]{0:T(1024)S(1)}, /*index=5*/f32[30...) all-reduce(f32[768]{0:T(1024)S(1)} %add.331, ...), channel_id=6, replica_groups=mesh['fsdp'=32] {'fsdp'}, use_global_device_ids=true, to_apply=%region_28.29.clone | all-reduce | flops 9216 | bytes 73728
  606.3 32.4 %reduce-scatter.23.cloned.1.call-done = f32[24,768]{1,0:T(8,128)} async-done(((f32[768,768]{1,0:T(8,128)}), f32[24,768]{1,0:T(8,128)}) %reduce-scatter.23.cloned.1.call-update) | async-done | bytes 73744
  638.8 103.9 %reduce-scatter.21.cloned.1.call-done = f32[24,768]{1,0:T(8,128)} async-done(((f32[768,768]{1,0:T(8,128)}), f32[24,768]{1,0:T(8,128)}) %reduce-scatter.21.cloned.1.call-update) | async-done | bytes 73744
  742.7 104.6 %reduce-scatter.19.cloned.1.call-done = f32[24,768]{1,0:T(8,128)} async-done(((f32[768,768]{1,0:T(8,128)}), f32[24,768]{1,0:T(8,128)}) %reduce-scatter.19.cloned.1.call-update) | async-done | bytes 73744
  847.3 141.1 %reduce-scatter.17.cloned.1.call-done = f32[96,768]{1,0:T(8,128)} async-done(((f32[3072,768]{1,0:T(8,128)}), f32[96,768]{1,0:T(8,128)}) %reduce-scatter.17.cloned.1.call-update) | async-done | bytes 294928 | tf_op jit(solution)/shard_map/reduce_scatter | solution.py:364
  988.5 141.8 %reduce-scatter.15.cloned.1.call-done = f32[24,3072]{1,0:T(8,128)} async-done(((f32[768,3072]{1,0:T(8,128)}), f32[24,3072]{1,0:T(8,128)}) %reduce-scatter.15.cloned.1.call-update) | async-done | bytes 294928 | tf_op jit(solution)/shard_map/reduce_scatter | solution.py:363
  (296 shorter events, 154.6 us)
Async XLA Ops:
  7.2 60.6 %all-gather.9.cloned.1.call-start = ((), (), s32[]{:S(2)}) async-start(), calls=%async_computation.7 | async-start | bytes 1216512 | tf_op jit(solution)/shard_map/all_gather | solution.py:285
  7.9 115.7 %all-gather.11.cloned.1.call-start = ((), (), s32[]{:S(2)}) async-start(), calls=%async_computation.8 | async-start | bytes 1216512 | tf_op jit(solution)/shard_map/all_gather | solution.py:286
  8.7 170.9 %all-gather.7.cloned.1.call-start = ((), (), s32[]{:S(2)}) async-start(), calls=%async_computation.6 | async-start | bytes 1216512 | tf_op jit(solution)/shard_map/all_gather | solution.py:287
  9.4 225.9 %all-gather.13.cloned.1.call-start = ((), (), s32[]{:S(2)}) async-start(), calls=%async_computation.9 | async-start | bytes 1216512 | tf_op jit(solution)/shard_map/all_gather | solution.py:288
  10.0 290.7 %all-gather.15.cloned.1.call-start = ((), (), s32[]{:S(2)}) async-start(), calls=%async_computation.10 | async-start | bytes 4866048 | tf_op jit(solution)/shard_map/all_gather | solution.py:296
  10.6 355.3 %all-gather.17.cloned.1.call-start = ((), (), s32[]{:S(2)}) async-start(), calls=%async_computation.11 | async-start | bytes 4866048 | tf_op jit(solution)/shard_map/all_gather | solution.py:297
  11.1 595.2 %reduce-scatter.13.cloned.1.call-start = ((), (), s32[]{:S(2)}) async-start(), calls=%async_computation.12 | async-start | bytes 2433024 | tf_op jit(solution)/shard_map/reduce_scatter | solution.py:355
  67.7 56.0 %copy-start.4 = (bf16[1024,768]{1,0:T(8,128)(2,1)S(1)}, bf16[1024,768]{1,0:T(8,128)(2,1)}, u32[]{:S(2)}) copy-start(bf16[1024,768]{1,0:T(8,128)(2,1)} %param.18) | copy-start | bytes 4718596
  70.4 114.4 %copy-start.19 = (bf16[512,768]{0,1:T(8,128)(2,1)}, bf16[512,768]{0,1:T(8,128)(2,1)S(1)}, u32[]{:S(2)}) copy-start(bf16[512,768]{0,1:T(8,128)(2,1)S(1)} %copy.82) | copy-start | bytes 2359300
  128.0 56.8 %copy-start.10 = (bf16[512,768]{0,1:T(8,128)(2,1)}, bf16[512,768]{0,1:T(8,128)(2,1)S(1)}, u32[]{:S(2)}) copy-start(bf16[512,768]{0,1:T(8,128)(2,1)S(1)} %copy.83) | copy-start | bytes 2359300
  300.6 7.9 copy-start.59
  365.9 6.5 copy-start.29
  365.9 6.5 copy-start.60
  365.9 6.5 copy-start.67
  418.5 6.3 copy-start.6
  436.0 202.8 %reduce-scatter.23.cloned.1.call-start = ((), (), s32[]{:S(2)}) async-start(), calls=%async_computation.17 | async-start | bytes 2433024
  437.1 6.8 copy-start.14
  437.1 6.9 copy-start.52
  443.9 8.9 copy-start.15
  443.9 8.1 copy-start.5
  466.4 9.8 copy-start.21
  479.2 263.6 %reduce-scatter.21.cloned.1.call-start = ((), (), s32[]{:S(2)}) async-start(), calls=%async_computation.16 | async-start | bytes 2433024
  479.2 12.8 %slice-start = ((s8[12582912]{0:T(1024)(128)(4,1)}), s8[4194304]{0:T(1024)(128)(4,1)S(1)}, s32[]{:S(2)}) async-start(s8[12582912]{0:T(1024)(128)(4,1)} %bitcast.137), calls=%async_computation.18 | async-start | bytes 8388608
  481.3 10.7 slice-start.1
  481.3 11.6 %slice-start.2 = ((s8[12582912]{0:T(1024)(128)(4,1)}), s8[4194304]{0:T(1024)(128)(4,1)S(1)}, s32[]{:S(2)}) async-start(s8[12582912]{0:T(1024)(128)(4,1)} %bitcast.137), calls=%async_computation.20 | async-start | bytes 8388608
  492.9 7.0 copy-start.20
  508.8 338.5 %reduce-scatter.19.cloned.1.call-start = ((), (), s32[]{:S(2)}) async-start(), calls=%async_computation.15 | async-start | bytes 2433024
  525.3 463.1 %reduce-scatter.17.cloned.1.call-start = ((), (), s32[]{:S(2)}) async-start(), calls=%async_computation.14 | async-start | bytes 9732096 | tf_op jit(solution)/shard_map/reduce_scatter | solution.py:364
  536.6 593.7 %reduce-scatter.15.cloned.1.call-start = ((), (), s32[]{:S(2)}) async-start(), calls=%async_computation.13 | async-start | bytes 9732096 | tf_op jit(solution)/shard_map/reduce_scatter | solution.py:363
  548.8 46.5 %copy-start.23 = (bf16[12,64,512]{2,1,0:T(8,128)(2,1)S(1)}, bf16[12,64,512]{2,1,0:T(8,128)(2,1)}, u32[]{:S(2)}) copy-start(bf16[12,64,512]{2,1,0:T(8,128)(2,1)} %copy-done.22) | copy-start | bytes 2359300
  548.8 46.5 %copy-start.62 = (bf16[768,768]{1,0:T(8,128)(2,1)S(1)}, bf16[768,768]{1,0:T(8,128)(2,1)}, u32[]{:S(2)}) copy-start(bf16[768,768]{1,0:T(8,128)(2,1)} %all-gather.9.cloned.1.call-done) | copy-start | bytes 3538948
  548.8 47.3 %copy-start.43 = (bf16[12,64,512]{2,1,0:T(8,128)(2,1)S(1)}, bf16[12,64,512]{2,1,0:T(8,128)(2,1)}, u32[]{:S(2)}) copy-start(bf16[12,64,512]{2,1,0:T(8,128)(2,1)} %copy-done.42) | copy-start | bytes 2359300
  (52 other events, 137.7 us)
Sparse Core Ops, SparseCore 0:
  10.9 56.7 all-gather.8
  70.6 52.9 all-gather.10
  126.5 52.9 all-gather.6
  182.3 52.9 all-gather.12
  238.1 62.5 all-gather.14
  303.4 62.4 all-gather.16
  436.1 97.8 reduce-scatter.12
  540.7 98.0 reduce-scatter.22
  644.7 97.9 reduce-scatter.20
  749.3 98.0 reduce-scatter.18
  853.8 134.5 reduce-scatter.16
  995.8 134.4 reduce-scatter.14
where the time goes:
time: 1150 us; the launch traced here: 1140 us
  waiting for transfers between devices  727 us (63%)
  matrix products  208 us (18%)
  blocking collectives  83.6 us (7%)
  local copies, waits for them, and re-layouts  67.3 us (6%)
  other arithmetic  35.6 us (3%)
  between operations  15.6 us (1%)
    unnamed x15, waiting for transfers between devices  245 us
    reduce_scatter x1, waiting for transfers between devices, shards(): lax.psum_scatter(up_weight_sum, 'fsdp', scatter_dimension=0, tiled=True)  142 us
    reduce_scatter x1, waiting for transfers between devices, shards(): lax.psum_scatter(down_weight_sum, 'fsdp', scatter_dimension=0, tiled=True)  141 us
    unnamed x2, blocking collectives  83.6 us
    dot_general x12, matrix products, times_plain(): return jnp.dot(left_side, right_side, preferred_element_type=jnp.float32)  68.5 us
    all_gather x1, waiting for transfers between devices, shards(): lax.all_gather(key_weight, 'fsdp', axis=0, tiled=True)  53.2 us
    all_gather x1, waiting for transfers between devices, shards(): lax.all_gather(value_weight, 'fsdp', axis=0, tiled=True)  51.6 us
    unnamed x174, local copies, waits for them, and re-layouts  50.3 us
  transfers between devices with their start and end apart: 12, of which 11 were waited for; matrix products, arithmetic and copies ran while one was open for 19% of the time, Pallas kernels for 0%

commit v1 on v0

--- a/solution.py
+++ b/solution.py
@@ -6,9 +6,6 @@
 from jax.sharding import PartitionSpec as P
 
 HEAD_DIM = 64
-MICRO = 2
-
-
 NEGATIVE = -1e30
 EPSILON = 1e-06
 
@@ -226,10 +223,24 @@
     return (input_grad, attention_terms, feed_terms)
 
 
-def add_terms(running, fresh):
-    if running is None:
-        return fresh
-    return tuple((left_side + right_side for left_side, right_side in zip(running, fresh)))
+def pack_rows(pieces, vectors, width, dtype):
+    blocks = pieces[0].shape[0]
+    line = jnp.concatenate([vector.astype(dtype) for vector in vectors], axis=1)
+    used = sum(piece.shape[1] for piece in pieces)
+    line_rows = -(-line.shape[1] // width)
+    line_rows += -(used + line_rows) % 16
+    line = jnp.pad(line, ((0, 0), (0, line_rows * width - line.shape[1])))
+    line = line.reshape(blocks, line_rows, width)
+    return jnp.concatenate([piece.astype(dtype) for piece in pieces] + [line], axis=1)
+
+
+def cut_line(line, lengths_of):
+    parts = []
+    start = 0
+    for length in lengths_of:
+        parts.append(line[:, start : start + length])
+        start += length
+    return parts
 
 
 def shards(
@@ -252,139 +263,110 @@
     second_shift,
     cotangent,
 ):
-
-    def fetch_backward():
-        feed_full = (
-            lax.all_gather(up_weight, "fsdp", axis=0, tiled=True),
-            lax.all_gather(down_weight, "fsdp", axis=0, tiled=True),
-            lax.all_gather(up_bias, "fsdp", axis=0, tiled=True),
-            lax.all_gather(down_bias, "fsdp", axis=0, tiled=True),
-            lax.all_gather(second_gain, "fsdp", axis=0, tiled=True),
-            lax.all_gather(second_shift, "fsdp", axis=0, tiled=True),
-        )
-        attention_full = (
-            lax.all_gather(query_weight, "fsdp", axis=0, tiled=True),
-            lax.all_gather(key_weight, "fsdp", axis=0, tiled=True),
-            lax.all_gather(value_weight, "fsdp", axis=0, tiled=True),
-            lax.all_gather(out_weight, "fsdp", axis=0, tiled=True),
-            lax.all_gather(query_bias, "fsdp", axis=0, tiled=True),
-            lax.all_gather(value_bias, "fsdp", axis=0, tiled=True),
-            lax.all_gather(out_bias, "fsdp", axis=0, tiled=True),
-            lax.all_gather(first_gain, "fsdp", axis=0, tiled=True),
-            lax.all_gather(first_shift, "fsdp", axis=0, tiled=True),
-        )
-        return (attention_full, feed_full)
-
-    micro_count = MICRO
-    micro_rows = tokens.shape[0] // micro_count
-    micro_slots = lengths.shape[0] // micro_count
-    outputs = []
-    stored_list = []
-    for micro_index in range(micro_count):
-        fetch_attention_full = (
-            lax.all_gather(query_weight, "fsdp", axis=0, tiled=True),
-            lax.all_gather(key_weight, "fsdp", axis=0, tiled=True),
-            lax.all_gather(value_weight, "fsdp", axis=0, tiled=True),
-            lax.all_gather(out_weight, "fsdp", axis=0, tiled=True),
-            lax.all_gather(query_bias, "fsdp", axis=0, tiled=True),
-            lax.all_gather(value_bias, "fsdp", axis=0, tiled=True),
-            lax.all_gather(out_bias, "fsdp", axis=0, tiled=True),
-            lax.all_gather(first_gain, "fsdp", axis=0, tiled=True),
-            lax.all_gather(first_shift, "fsdp", axis=0, tiled=True),
-        )
-        fetch_feed_full = (
-            lax.all_gather(up_weight, "fsdp", axis=0, tiled=True),
-            lax.all_gather(down_weight, "fsdp", axis=0, tiled=True),
-            lax.all_gather(up_bias, "fsdp", axis=0, tiled=True),
-            lax.all_gather(down_bias, "fsdp", axis=0, tiled=True),
-            lax.all_gather(second_gain, "fsdp", axis=0, tiled=True),
-            lax.all_gather(second_shift, "fsdp", axis=0, tiled=True),
-        )
-        attention_full = fetch_attention_full
-        feed_full = fetch_feed_full
-        row_start = micro_index * micro_rows
-        slot_start = micro_index * micro_slots
-        output, stored = forward_pass(
-            tokens[row_start : row_start + micro_rows],
-            lengths[slot_start : slot_start + micro_slots],
-            attention_full,
-            feed_full,
-        )
-        outputs.append(output)
-        stored_list.append(stored)
-    input_grads = [None] * micro_count
-    attention_total = None
-    feed_total = None
-    attention_owned = None
-    feed_owned = None
-    for micro_index in reversed(range(micro_count)):
-        attention_full, feed_full = fetch_backward()
-        row_start = micro_index * micro_rows
-        input_grad, attention_terms, feed_terms = backward_pass(
-            stored_list[micro_index],
-            cotangent[row_start : row_start + micro_rows],
-            attention_full,
-            feed_full,
-        )
-        input_grads[micro_index] = input_grad
-        attention_total = add_terms(attention_total, attention_terms)
-        feed_total = add_terms(feed_total, feed_terms)
-    (
-        query_weight_sum,
-        key_weight_sum,
-        value_weight_sum,
-        out_weight_sum,
-        query_bias_sum,
-        value_bias_sum,
-        out_bias_sum,
-        first_gain_sum,
-        first_shift_sum,
-    ) = attention_total
-    (
-        up_weight_sum,
-        down_weight_sum,
-        up_bias_sum,
-        down_bias_sum,
-        second_gain_sum,
-        second_shift_sum,
-    ) = feed_total
-    attention_owned = (
-        lax.psum_scatter(query_weight_sum, "fsdp", scatter_dimension=0, tiled=True),
-        lax.psum_scatter(key_weight_sum, "fsdp", scatter_dimension=0, tiled=True),
-        lax.psum_scatter(value_weight_sum, "fsdp", scatter_dimension=0, tiled=True),
-        lax.psum_scatter(out_weight_sum, "fsdp", scatter_dimension=0, tiled=True),
-        lax.psum_scatter(query_bias_sum, "fsdp", scatter_dimension=0, tiled=True),
-        lax.psum_scatter(value_bias_sum, "fsdp", scatter_dimension=0, tiled=True),
-        lax.psum_scatter(out_bias_sum, "fsdp", scatter_dimension=0, tiled=True),
-        lax.psum_scatter(first_gain_sum, "fsdp", scatter_dimension=0, tiled=True),
-        lax.psum_scatter(first_shift_sum, "fsdp", scatter_dimension=0, tiled=True),
-    )
-    feed_owned = (
-        lax.psum_scatter(up_weight_sum, "fsdp", scatter_dimension=0, tiled=True),
-        lax.psum_scatter(down_weight_sum, "fsdp", scatter_dimension=0, tiled=True),
-        lax.psum_scatter(up_bias_sum, "fsdp", scatter_dimension=0, tiled=True),
-        lax.psum_scatter(down_bias_sum, "fsdp", scatter_dimension=0, tiled=True),
-        lax.psum_scatter(second_gain_sum, "fsdp", scatter_dimension=0, tiled=True),
-        lax.psum_scatter(second_shift_sum, "fsdp", scatter_dimension=0, tiled=True),
-    )
+    own_rows, width = query_weight.shape
+    feed_rows = down_weight.shape[0]
+    fold = up_weight.shape[1] // width
+    device_count = width // own_rows
+    feed_width = feed_rows * device_count
+
+    def up_pieces(matrix, blocks):
+        return [
+            matrix[:, part * width : (part + 1) * width].reshape(blocks, -1, width)
+            for part in range(fold)
+        ]
+
+    vectors = (
+        query_bias,
+        value_bias,
+        out_bias,
+        first_gain,
+        first_shift,
+        down_bias,
+        second_gain,
+        second_shift,
+        up_bias,
+    )
+    packed = pack_rows(
+        [query_weight[None], key_weight[None], value_weight[None], out_weight[None]]
+        + up_pieces(up_weight, 1)
+        + [down_weight[None]],
+        [vector[None] for vector in vectors],
+        width,
+        jnp.bfloat16,
+    )
+    gathered = lax.all_gather(packed[0], "fsdp", axis=0, tiled=False)
+    square = [
+        gathered[:, part * own_rows : (part + 1) * own_rows].reshape(width, width)
+        for part in range(4 + fold)
+    ]
+    down_start = (4 + fold) * own_rows
+    down_full = gathered[:, down_start : down_start + feed_rows].reshape(feed_width, width)
+    line = gathered[:, down_start + feed_rows :].reshape(device_count, -1)
+    lines = cut_line(line, [vector.shape[0] for vector in vectors])
+    lines = [part.reshape(-1) for part in lines]
+    attention_full = tuple(square[:4]) + tuple(lines[:5])
+    feed_full = (
+        jnp.concatenate(square[4:], axis=1),
+        down_full,
+        lines[8],
+        lines[5],
+        lines[6],
+        lines[7],
+    )
+
+    output, stored = forward_pass(tokens, lengths, attention_full, feed_full)
+    input_grad, attention_terms, feed_terms = backward_pass(
+        stored, cotangent, attention_full, feed_full
+    )
+
+    def to_blocks(matrix):
+        return matrix.reshape(device_count, -1, width)
+
+    def to_lines(vector):
+        return vector.reshape(device_count, -1)
+
+    up_term, down_term, up_bias_term, down_bias_term, gain_term, shift_term = feed_terms
+    feed_packed = pack_rows(
+        up_pieces(up_term, device_count) + [to_blocks(down_term)],
+        [to_lines(part) for part in (up_bias_term, down_bias_term, gain_term, shift_term)],
+        width,
+        jnp.bfloat16,
+    )
+    feed_owned = lax.psum_scatter(
+        feed_packed.reshape(-1, width), "fsdp", scatter_dimension=0, tiled=True
+    )
+    attention_packed = pack_rows(
+        [to_blocks(part) for part in attention_terms[:4]],
+        [to_lines(part) for part in attention_terms[4:]],
+        width,
+        jnp.bfloat16,
+    )
+    attention_owned = lax.psum_scatter(
+        attention_packed.reshape(-1, width), "fsdp", scatter_dimension=0, tiled=True
+    )
+    feed_owned = feed_owned.astype(jnp.float32)
+    attention_owned = attention_owned.astype(jnp.float32)
+    up_owned = jnp.concatenate(
+        [feed_owned[part * own_rows : (part + 1) * own_rows] for part in range(fold)], axis=1
+    )
+    down_owned = feed_owned[fold * own_rows : fold * own_rows + feed_rows]
+    feed_line = feed_owned[fold * own_rows + feed_rows :].reshape(1, -1)
+    feed_vectors = [
+        part[0] for part in cut_line(feed_line, [feed_rows, own_rows, own_rows, own_rows])
+    ]
+    squares_owned = [
+        attention_owned[part * own_rows : (part + 1) * own_rows] for part in range(4)
+    ]
+    attention_line = attention_owned[4 * own_rows :].reshape(1, -1)
+    attention_vectors = [part[0] for part in cut_line(attention_line, [own_rows] * 5)]
     return (
-        jnp.concatenate(outputs, axis=0),
-        jnp.concatenate(input_grads, axis=0),
-        attention_owned[0],
-        attention_owned[1],
-        attention_owned[2],
-        attention_owned[3],
-        attention_owned[4],
-        attention_owned[5],
-        attention_owned[6],
-        attention_owned[7],
-        attention_owned[8],
-        feed_owned[0],
-        feed_owned[1],
-        feed_owned[2],
-        feed_owned[3],
-        feed_owned[4],
-        feed_owned[5],
+        output,
+        input_grad,
+        *squares_owned,
+        *attention_vectors,
+        up_owned,
+        down_owned,
+        *feed_vectors,
     )
 
 

time: 1150 us -> 671 us (0.58)
  waiting for transfers between devices: 727 us -> 319 us
  blocking collectives: 83.6 us -> 0 us
  local copies, waits for them, and re-layouts: 67.3 us -> 85.9 us
    unnamed x15 -> x3, waiting for transfers between devices: 245 us -> 0.05 us
    all_gather x6 -> x1, waiting for transfers between devices: 199 us -> 104 us  [shards(): gathered = lax.all_gather(packed[0], 'fsdp', axis=0, tiled=False)]
    unnamed x2 -> x0, blocking collectives: 83.6 us -> none
    reduce_scatter x3 -> x2, waiting for transfers between devices: 283 us -> 215 us  [the longest x1 142 us: shards(): lax.psum_scatter(feed_packed.reshape(-1, width), 'fsdp', scatter_dimensio...]
    reshape x0 -> x5, local copies, waits for them, and re-layouts: none -> 13.6 us  [the longest x4 13.6 us: split_heads(): matrix.reshape(slot_count, row_count // slot_count, model_width // HEAD_D...]
    slice x1 -> x7, local copies, waits for them, and re-layouts: 1.31 us -> 14.8 us  [the longest x1 6.64 us: shards(): gathered[:, part * own_rows:(part + 1) * own_rows].reshape(width, width)]
    dot_general x12 -> x6, matrix products: 37.2 us -> 23.8 us  [times_across(): lax.dot_general(left_side, right_side, (((0,), (0,)), ((), ())), preferre...]
    unnamed x174 -> x131, local copies, waits for them, and re-layouts: 50.3 us -> 38.5 us
  transfers between devices with their start and end apart: 12 -> 3, of which waited for: 11 -> 3; matrix products, arithmetic and copies ran while one was open for 19% -> 7% of each run, Pallas kernels for 0% -> 0%
where the time goes in v1:
time: 671 us; the launch traced here: 661 us
  waiting for transfers between devices  319 us (48%)
  matrix products  197 us (29%)
  local copies, waits for them, and re-layouts  85.9 us (13%)
  other arithmetic  44.1 us (7%)
  between operations  15.1 us (2%)
    reduce_scatter x1, waiting for transfers between devices, shards(): lax.psum_scatter(feed_packed.reshape(-1, width), 'fsdp', scatter_dimensio...  142 us
    all_gather x1, waiting for transfers between devices, shards(): gathered = lax.all_gather(packed[0], 'fsdp', axis=0, tiled=False)  104 us
    reduce_scatter x1, waiting for transfers between devices, shards(): lax.psum_scatter(attention_packed.reshape(-1, width), 'fsdp', scatter_dim...  72.6 us
    dot_general x6, matrix products, times_plain(): return jnp.dot(left_side, right_side, preferred_element_type=jnp.float32)  61.1 us
    dot_general x6, matrix products, times_back(): lax.dot_general(left_side, right_side, (((1,), (1,)), ((), ())), preferre...  39.2 us
    unnamed x131, local copies, waits for them, and re-layouts  38.5 us
    dot_general x6, matrix products, times_across(): lax.dot_general(left_side, right_side, (((0,), (0,)), ((), ())), preferre...  23.8 us
    convert_element_type x1, other arithmetic, backward_pass(): grad_scores = (probs * (grad_probs - row_delta)).astype(jnp.bfloat16)  21.8 us
  transfers between devices with their start and end apart: 3, of which 3 were waited for; matrix products, arithmetic and copies ran while one was open for 7% of the time, Pallas kernels for 0%

profile of v1, /device:TPU:0, one launch (start us, length us, event | category | flops | bytes accessed | tf_op | source)
XLA Modules:
  0.0 660.9 jit_solution(9417903419846546755)
XLA Ops:
  21.8 103.8 %all-gather.2.cloned.1.call-done = bf16[32,304,768]{2,1,0:T(8,128)(2,1)} async-done(((bf16[1,304,768]{2,1,0:T(8,128)(2,1)}), bf16[32,304,768]{2,1,0:T(8,128)(2,1)}) %all-gather.2.cloned.1.call-update) | async-done | bytes 14942224 | tf_op jit(solution)/shard_map/all_gather | solution.py:297
  129.8 6.6 %fusion.70 = (bf16[32,24,768]{2,1,0:T(8,128)(2,1)}, bf16[32,24,768]{2,1,0:T(8,128)(2,1)}, bf16[32,24,768]{2,1,0:T(8,128)(2,1)}, bf16[32,24,768]{2,1,0:T(8,128)(2...) fusion(bf16[32,304,768]{2,1,0:T(8,128)(2,1)} %all-gather.2.clon, ...), kind=kLoop, calls=%fused_computation.158 | loop fusion | bytes 18874368 | tf_op jit(solution)/shard_map/slice | solution.py:299
  137.5 2.7 fusion.39
  140.1 2.9 reshape.357
  143.0 4.6 fusion.38
  147.7 4.0 reshape.355
  151.7 3.8 fusion.37
  155.5 2.9 reshape.359
  158.4 11.1 %fusion.12 = (f32[2,12,512]{2,1,0:T(8,128)S(1)}, f32[2,12,512,512]{2,3,1,0:T(8,128)}) fusion(pred[2,512]{1,0:T(4,128)(4,1)S(1)} %get-tuple-element.124, bf16[2,512,12,64]{1,0,3,2:T(2,128)(2,1)S(1)} %reshape.359, bf16[2,512,12,64]{1,0,3,2:T(2,128)(2,1)S(1)} %reshape.357), kind=kOutput, calls=%fused_computation.28 | convolution fusion | flops 824168448 | bytes 28361728 | tf_op jit(solution)/shard_map/sqhd,skhd->shqk/dot_general | solution.py:53
  169.5 11.2 %fusion = f32[2,12,512]{2,1,0:T(8,128)S(1)} fusion(f32[2,12,512]{2,1,0:T(8,128)S(1)} %get-tuple-element.125, f32[2,12,512,512]{2,3,1,0:T(8,128)} %get-tuple-element.126, pred[2,512]{1,0:T(4,128)(4,1)S(1)} %get-tuple-element.124), kind=kLoop, calls=%fused_computation.6 | loop fusion | flops 25153536 | bytes 25265152 | tf_op jit(solution)/shard_map/reduce_sum | solution.py:87
  181.4 11.8 %fusion.40 = bf16[2,512,12,64]{1,3,2,0:T(8,128)(2,1)S(1)} fusion(f32[2,12,512]{2,1,0:T(8,128)S(1)} %fusion, f32[2,12,512]{2,1,0:T(8,128)S(1)} %get-tuple-element.125, f32[2,12,512,512]{2,3,1,0:T(8,128)} %get-tuple-element.126, pred[2,512]{1,0:T(4,128)(4,1)S(1)} %get-tuple-element.124, bf16[2,512,12,64]{1,0,3,2:T(2,128)(2,1)S(1)} %copy-done.10), kind=kOutput, calls=%fused_computation.78 | convolution fusion | flops 837550080 | bytes 28410880 | tf_op jit(solution)/shard_map/shqk,skhd->sqhd/dot_general | solution.py:90
  199.8 38.9 %multiply_convert_fusion.1 = (bf16[1024,3072]{1,0:T(8,128)(2,1)}, f32[1024,3072]{1,0:T(8,128)}, f32[1024,3072]{1,0:T(8,128)}) fusion(f32[3072]{0:T(1024)S(1)} %reshape.378, bf16[768,768]{1,0:T(8,128)(2,1)S(1)} %bitcast.208, bf16[768,768]{1,0:T(8,128)(2,1)S(1)} %bitcast.210, bf16[768,768]{1,0:T(8,128)(2,1)S(1)} %bitcast.212, ...), kind=kOutput, calls=%fused_computation.13 | convolution fusion | flops 5062262784 | bytes 39348224 | tf_op jit(solution)/shard_map/dot_general | solution.py:24
  238.8 2.7 slice.207
  241.5 9.4 %fusion.75 = (f32[1024]{0:T(1024)S(1)}, f32[1024,768]{0,1:T(8,128)S(1)}) fusion(f32[768]{0:T(1024)S(1)} %copy-done.46, bf16[1024,3072]{1,0:T(8,128)(2,1)} %get-tuple-element.82, bf16[3072,768]{1,0:T(8,128)(2,1)S(1)} %bitcast.185, f32[768]{0:T(1024)S(1)} %reshape.377, f32[768]{0:T(1024)S(1)} %reshape.376, f32[1024]{0:T(1024)S(1)} %fusion.55, ...), kind=kOutput, calls=%fused_computation.163 | convolution fusion | flops 4837342208 | bytes 17323008 | tf_op jit(solution)/shard_map/dot_general | solution.py:24
  251.8 3.1 multiply_reduce_fusion.1
  256.2 17.5 %fusion.78 = (bf16[3072]{0:T(1024)(128)(2,1)S(1)}, bf16[1024,3072]{1,0:T(8,128)(2,1)}) fusion(f32[1024,3072]{1,0:T(8,128)} %get-tuple-element.83, bf16[1024,768]{0,1:T(8,128)(2,1)S(1)} %get-tuple-element.77, bf16[3072,768]{1,0:T(8,128)(2,1)} %bitcast.186, f32[1024,3072]{1,0:T(8,128)} %get-tuple-element.129, f32[3072]{0:T(1024)S(1)} %reshape.378), kind=kOutput, calls=%fused_computation.166 | convolution fusion | flops 4882166784 | bytes 37767168 | tf_op jit(solution)/shard_map/dot_general | solution.py:34
  273.8 11.7 %multiply_reduce_fusion.2 = (bf16[768]{0:T(1024)(128)(2,1)S(1)}, f32[1024]{0:T(1024)S(1)}, bf16[768]{0:T(1024)(128)(2,1)S(1)}, f32[1024,768]{0,1:T(8,128)S(1)}) fusion(f32[1024,768]{0,1:T(8,128)} %copy-done.5, f32[1024]{0:T(1024)S(1)} %fusion.55, f32[1024]{0:T(1024)S(1)} %broadcast_multiply_fusion.1, f32[768]{0:T(1024)S(1)} %reshape.376, ...), kind=kOutput, calls=%fused_computation.35 | convolution fusion | flops 4864865280 | bytes 22062080 | tf_op jit(solution)/shard_map/dot_general | solution.py:34
  290.5 2.7 copy.90
  293.2 3.8 reshape.366
  297.0 12.5 %fusion.77 = (bf16[12,64]{1,0:T(8,128)(2,1)S(1)}, bf16[2,512,12,64]{1,3,2,0:T(8,128)(2,1)}) fusion(f32[2,12,512]{2,1,0:T(8,128)S(1)} %copy-done.37, f32[2,12,512,512]{2,3,1,0:T(8,128)} %get-tuple-element.126, pred[2,512]{1,0:T(4,128)(4,1)S(1)} %copy-done.40, bf16[2,512,12,64]{1,0,3,2:T(2,128)(2,1)} %reshape.366), kind=kOutput, calls=%fused_computation.165 | convolution fusion | flops 832044288 | bytes 28363264 | tf_op jit(solution)/shard_map/shqk,sqhd->skhd/dot_general | solution.py:177
  309.5 19.8 %multiply_reduce_fusion = (f32[2,12,512]{2,1,0:T(8,128)S(1)}, f32[2,12,512,512]{2,3,1,0:T(8,128)}) fusion(f32[2,12,512]{2,1,0:T(8,128)S(1)} %copy-done.37, f32[2,12,512,512]{2,3,1,0:T(8,128)} %get-tuple-element.126, pred[2,512]{1,0:T(4,128)(4,1)S(1)} %copy-done.40, bf16[2,512,12,64]{1,0,3,2:T(2,128)(2,1)} %reshape.355, bf16[2,512,12,64]{1,0,3,2:T(2,128)(2,1)} %reshape.366), kind=kOutput, calls=%fused_computation.1 | convolution fusion | flops 836751360 | bytes 53576704 | tf_op jit(solution)/shard_map/sqhd,skhd->shqk/dot_general | solution.py:174
  329.3 21.8 %multiply_convert_fusion = bf16[2,12,512,512]{2,3,1,0:T(8,128)(2,1)} fusion(f32[2,12,512,512]{2,3,1,0:T(8,128)} %get-tuple-element.134, f32[2,12,512]{2,1,0:T(8,128)S(1)} %get-tuple-element.133, f32[2,12,512]{2,1,0:T(8,128)S(1)} %copy-done.37, f32[2,12,512,512]{2,3,1,0:T(8,128)} %get-tuple-element.126, pred[2,512]{1,0:T(4,128)(4,1)S(1)} %copy-done.40), kind=kLoop, calls=%fused_computation | loop fusion | flops 37748736 | bytes 63013888 | tf_op jit(solution)/shard_map/convert_element_type | solution.py:185
  351.0 9.7 %fusion.36 = bf16[2,512,12,64]{1,3,2,0:T(8,128)(2,1)} fusion(bf16[2,12,512,512]{2,3,1,0:T(8,128)(2,1)} %multiply_convert_fusion, bf16[2,512,12,64]{1,0,3,2:T(2,128)(2,1)S(1)} %copy-done.4), kind=kOutput, calls=%fused_computation.74 | convolution fusion | flops 806879232 | bytes 15728640 | tf_op jit(solution)/shard_map/shqk,sqhd->skhd/dot_general | solution.py:191
  360.8 7.9 %fusion.76 = (bf16[12,64]{1,0:T(8,128)(2,1)S(1)}, bf16[2,512,12,64]{1,3,2,0:T(8,128)(2,1)}) fusion(bf16[2,12,512,512]{2,3,1,0:T(8,128)(2,1)} %multiply_convert_fusion, bf16[2,512,12,64]{1,0,3,2:T(2,128)(2,1)S(1)} %copy-done.2), kind=kOutput, calls=%fused_computation.164 | convolution fusion | flops 807664896 | bytes 15730176 | tf_op jit(solution)/shard_map/shqk,skhd->sqhd/dot_general | solution.py:187
  369.1 3.1 copy.103
  379.9 3.4 convolution_convert_fusion.5
  394.9 8.3 %convolution_convert_fusion.1 = bf16[768,3072]{1,0:T(8,128)(2,1)S(1)} fusion(bf16[1024,3072]{1,0:T(8,128)(2,1)} %get-tuple-element.140, f32[1024,768]{0,1:T(8,128)} %copy-done.5, f32[768]{0:T(1024)S(1)} %reshape.377, f32[768]{0:T(1024)S(1)} %reshape.376, f32[1024]{0:T(1024)S(1)} %fusion.55, f32[1024]{0:T(1024)S(1)} %broadcast_multiply_fusion.1), kind=kOutput, calls=%fused_computation.30 | convolution fusion | flops 4838129664 | bytes 14170112 | tf_op jit(solution)/shard_map/dot_general | solution.py:28
  408.4 5.5 convolution_convert_fusion
  420.0 3.4 fusion.80
  425.2 2.6 add_convert_fusion.1
  430.4 72.6 %reduce-scatter.3.cloned.1.call-done = bf16[112,768]{1,0:T(8,128)(2,1)} async-done(((bf16[3584,768]{1,0:T(8,128)(2,1)}), bf16[112,768]{1,0:T(8,128)(2,1)}) %reduce-scatter.3.cloned.1.call-update) | async-done | bytes 172048 | tf_op jit(solution)/shard_map/reduce_scatter | solution.py:344
  506.2 142.4 %reduce-scatter.5.cloned.1.call-done = bf16[208,768]{1,0:T(8,128)(2,1)} async-done(((bf16[6656,768]{1,0:T(8,128)(2,1)}), bf16[208,768]{1,0:T(8,128)(2,1)}) %reduce-scatter.5.cloned.1.call-update) | async-done | bytes 319504 | tf_op jit(solution)/shard_map/reduce_scatter | solution.py:335
  (201 shorter events, 77.7 us)
Async XLA Ops:
  7.2 13.0 %copy-start.17 = (bf16[1024,768]{1,0:T(8,128)(2,1)S(1)}, bf16[1024,768]{1,0:T(8,128)(2,1)}, u32[]{:S(2)}) copy-start(bf16[1024,768]{1,0:T(8,128)(2,1)} %param.18) | copy-start | bytes 4718596
  7.2 118.4 %all-gather.2.cloned.1.call-start = ((), (), s32[]{:S(2)}) async-start(), calls=%async_computation.2 | async-start | bytes 15409152 | tf_op jit(solution)/shard_map/all_gather | solution.py:297
  16.2 486.8 %reduce-scatter.3.cloned.1.call-start = ((), (), s32[]{:S(2)}) async-start(), calls=%async_computation.3 | async-start | bytes 5677056 | tf_op jit(solution)/shard_map/reduce_scatter | solution.py:344
  17.0 164.4 %copy-start.39 = (pred[2,512]{1,0:T(4,128)(4,1)}, pred[2,512]{1,0:T(4,128)(4,1)S(1)}, u32[]{:S(2)}) copy-start(pred[2,512]{1,0:T(4,128)(4,1)S(1)} %get-tuple-element.124) | copy-start | bytes 3076
  136.4 6.6 copy-start.12
  143.0 15.4 %copy-start.3 = (bf16[2,512,12,64]{1,0,3,2:T(2,128)(2,1)}, bf16[2,512,12,64]{1,0,3,2:T(2,128)(2,1)S(1)}, u32[]{:S(2)}) copy-start(bf16[2,512,12,64]{1,0,3,2:T(2,128)(2,1)S(1)} %reshape.357) | copy-start | bytes 4718596
  147.7 4.0 copy-start.18
  158.4 11.1 %copy-start.1 = (bf16[2,512,12,64]{1,0,3,2:T(2,128)(2,1)}, bf16[2,512,12,64]{1,0,3,2:T(2,128)(2,1)S(1)}, u32[]{:S(2)}) copy-start(bf16[2,512,12,64]{1,0,3,2:T(2,128)(2,1)S(1)} %reshape.359) | copy-start | bytes 4718596
  169.5 11.9 %copy-start.10 = (bf16[2,512,12,64]{1,0,3,2:T(2,128)(2,1)S(1)}, bf16[2,512,12,64]{1,0,3,2:T(2,128)(2,1)}, u32[]{:S(2)}) copy-start(bf16[2,512,12,64]{1,0,3,2:T(2,128)(2,1)} %reshape.355) | copy-start | bytes 4718596
  196.9 44.5 %copy-start.5 = (f32[1024,768]{0,1:T(8,128)}, f32[1024,768]{0,1:T(8,128)S(1)}, u32[]{:S(2)}) copy-start(f32[1024,768]{0,1:T(8,128)S(1)} %get-tuple-element.128) | copy-start | bytes 9437188
  197.4 41.4 %copy-start.43 = (f32[1024]{0:T(1024)}, f32[1024]{0:T(1024)S(1)}, u32[]{:S(2)}) copy-start(f32[1024]{0:T(1024)S(1)} %multiply_reduce_fusion.6) | copy-start | bytes 12292
  241.4 9.5 %copy-start.14 = (bf16[32,96,768]{2,1,0:T(8,128)(2,1)}, bf16[32,96,768]{2,1,0:T(8,128)(2,1)S(1)}, u32[]{:S(2)}) copy-start(bf16[32,96,768]{2,1,0:T(8,128)(2,1)S(1)} %slice.207) | copy-start | bytes 14155780
  241.4 9.5 %copy-start = (bf16[1024,768]{0,1:T(8,128)(2,1)S(1)}, bf16[1024,768]{0,1:T(8,128)(2,1)}, u32[]{:S(2)}) copy-start(bf16[1024,768]{0,1:T(8,128)(2,1)} %copy.88) | copy-start | bytes 4718596
  241.5 9.5 %copy-start.41 = (f32[768]{0:T(1024)S(1)}, f32[768]{0:T(1024)}, u32[]{:S(2)}) copy-start(f32[768]{0:T(1024)} %reshape.380) | copy-start | bytes 9220
  241.5 9.5 %copy-start.42 = (f32[1,4,2,128]{3,1,2,0:T(4,128)S(1)}, f32[1,4,2,128]{3,1,2,0:T(4,128)}, u32[]{:S(2)}) copy-start(f32[1,4,2,128]{3,1,2,0:T(4,128)} %copy.120) | copy-start | bytes 12292
  256.2 17.5 %copy-start.26 = (bf16[1024,768]{0,1:T(8,128)(2,1)}, bf16[1024,768]{0,1:T(8,128)(2,1)S(1)}, u32[]{:S(2)}) copy-start(bf16[1024,768]{0,1:T(8,128)(2,1)S(1)} %get-tuple-element.77) | copy-start | bytes 4718596
  273.8 11.7 %copy-start.44 = (f32[1024]{0:T(1024)S(1)}, f32[1024]{0:T(1024)}, u32[]{:S(2)}) copy-start(f32[1024]{0:T(1024)} %copy-done.43) | copy-start | bytes 12292
  273.8 11.8 %copy-start.6 = (f32[1024,768]{0,1:T(8,128)S(1)}, f32[1024,768]{0,1:T(8,128)}, u32[]{:S(2)}) copy-start(f32[1024,768]{0,1:T(8,128)} %copy-done.5) | copy-start | bytes 9437188
  290.5 6.5 copy-start.37
  290.5 6.5 copy-start.40
  329.3 21.8 %copy-start.4 = (bf16[2,512,12,64]{1,0,3,2:T(2,128)(2,1)S(1)}, bf16[2,512,12,64]{1,0,3,2:T(2,128)(2,1)}, u32[]{:S(2)}) copy-start(bf16[2,512,12,64]{1,0,3,2:T(2,128)(2,1)} %copy-done.3) | copy-start | bytes 4718596
  351.0 9.8 %copy-start.2 = (bf16[2,512,12,64]{1,0,3,2:T(2,128)(2,1)S(1)}, bf16[2,512,12,64]{1,0,3,2:T(2,128)(2,1)}, u32[]{:S(2)}) copy-start(bf16[2,512,12,64]{1,0,3,2:T(2,128)(2,1)} %copy-done.1) | copy-start | bytes 4718596
  369.1 4.7 copy-start.19
  379.9 3.5 copy-start.7
  387.2 3.5 copy-start.16
  387.2 3.5 copy-start.22
  394.2 254.3 %reduce-scatter.5.cloned.1.call-start = ((), (), s32[]{:S(2)}) async-start(), calls=%async_computation.4 | async-start | bytes 10543104 | tf_op jit(solution)/shard_map/reduce_scatter | solution.py:335
  403.2 4.9 slice-start
  403.6 4.5 slice-start.1
  404.7 3.6 copy-start.27
  420.0 3.4 copy-start.24
  420.0 3.4 copy-start.29
  (20 other events, 36.6 us)
Sparse Core Ops, SparseCore 0:
  16.4 109.2 all-gather.1
  394.4 108.6 reduce-scatter.2
  510.1 138.4 reduce-scatter.4

commit v2 on v1

--- a/solution.py
+++ b/solution.py
@@ -17,7 +17,7 @@
 
 
 def gelu_exact(upward):
-    return jax.nn.gelu(upward, approximate=False)
+    return upward * (0.5 + 0.5 * lax.erf(upward * math.sqrt(0.5)))
 
 
 def times_plain(left_side, right_side):
@@ -223,6 +223,70 @@
     return (input_grad, attention_terms, feed_terms)
 
 
+def axis_sizes(device_count):
+    side = 1
+    while 2 * (2 * side) ** 3 <= device_count:
+        side *= 2
+    return (device_count // (2 * side * side), side, side, 2)
+
+
+def axis_digit(sizes, axis):
+    stride = math.prod(sizes[axis + 1 :])
+    return stride, (lax.axis_index("fsdp") // stride) % sizes[axis]
+
+
+def shifted_pairs(sizes, axis, shift):
+    stride = math.prod(sizes[axis + 1 :])
+    pairs = []
+    for index in range(math.prod(sizes)):
+        digit = (index // stride) % sizes[axis]
+        pairs.append((index, index + ((digit + shift) % sizes[axis] - digit) * stride))
+    return pairs
+
+
+def scatter_sum(blocks, sizes, order):
+    remaining = [0, 1, 2, 3]
+    held = blocks.reshape(sizes + blocks.shape[1:])
+    for axis in order:
+        place = remaining.index(axis)
+        _, digit = axis_digit(sizes, axis)
+        held = held.astype(jnp.bfloat16)
+        arrived = []
+        for shift in range(1, sizes[axis]):
+            target = (digit + shift) % sizes[axis]
+            part = lax.dynamic_index_in_dim(held, target, place, keepdims=False)
+            arrived.append(lax.ppermute(part, "fsdp", shifted_pairs(sizes, axis, shift)))
+        own = lax.dynamic_index_in_dim(held, digit, place, keepdims=False)
+        held = own.astype(jnp.float32)
+        for part in arrived:
+            held = held + part.astype(jnp.float32)
+        remaining.remove(axis)
+    return held
+
+
+def gather_blocks(own, sizes, order):
+    present = []
+    held = own
+    for axis in order:
+        place = sum(1 for other in present if other < axis)
+        _, digit = axis_digit(sizes, axis)
+        shape = held.shape[:place] + (sizes[axis],) + held.shape[place:]
+        joined = lax.dynamic_update_index_in_dim(
+            jnp.zeros(shape, held.dtype), held, digit, place
+        )
+        for shift in range(1, sizes[axis]):
+            part = lax.ppermute(held, "fsdp", shifted_pairs(sizes, axis, shift))
+            source = (digit - shift) % sizes[axis]
+            joined = lax.dynamic_update_index_in_dim(joined, part, source, place)
+        held = joined
+        present.append(axis)
+    return held.reshape((math.prod(sizes),) + own.shape)
+
+
+X_FIRST = (3, 2, 1, 0)
+Y_FIRST = (3, 1, 2, 0)
+
+
 def pack_rows(pieces, vectors, width, dtype):
     blocks = pieces[0].shape[0]
     line = jnp.concatenate([vector.astype(dtype) for vector in vectors], axis=1)
@@ -275,44 +339,48 @@
             for part in range(fold)
         ]
 
-    vectors = (
-        query_bias,
-        value_bias,
-        out_bias,
-        first_gain,
-        first_shift,
-        down_bias,
-        second_gain,
-        second_shift,
-        up_bias,
-    )
-    packed = pack_rows(
-        [query_weight[None], key_weight[None], value_weight[None], out_weight[None]]
-        + up_pieces(up_weight, 1)
-        + [down_weight[None]],
+    sizes = axis_sizes(device_count)
+
+    feed_vectors = (up_bias, down_bias, second_gain, second_shift)
+    feed_packed = pack_rows(
+        up_pieces(up_weight, 1) + [down_weight[None]],
+        [vector[None] for vector in feed_vectors],
+        width,
+        jnp.bfloat16,
+    )
+    gathered = lax.all_gather(feed_packed[0], "fsdp", axis=0, tiled=False)
+    up_full = jnp.concatenate(
+        [
+            gathered[:, part * own_rows : (part + 1) * own_rows].reshape(width, width)
+            for part in range(fold)
+        ],
+        axis=1,
+    )
+    down_start = fold * own_rows
+    down_full = gathered[:, down_start : down_start + feed_rows].reshape(feed_width, width)
+    line = gathered[:, down_start + feed_rows :].reshape(device_count, -1)
+    lines = cut_line(line, [vector.shape[0] for vector in feed_vectors])
+    feed_full = (up_full, down_full) + tuple(part.reshape(-1) for part in lines)
+
+    vectors = (query_bias, value_bias, out_bias, first_gain, first_shift)
+    near = pack_rows(
+        [query_weight[None], key_weight[None]],
         [vector[None] for vector in vectors],
         width,
         jnp.bfloat16,
     )
-    gathered = lax.all_gather(packed[0], "fsdp", axis=0, tiled=False)
+    near = gather_blocks(near[0], sizes, X_FIRST[::-1])
+    far = gather_blocks(
+        jnp.concatenate([value_weight, out_weight], axis=0), sizes, Y_FIRST[::-1]
+    )
     square = [
-        gathered[:, part * own_rows : (part + 1) * own_rows].reshape(width, width)
-        for part in range(4 + fold)
+        array[:, part * own_rows : (part + 1) * own_rows].reshape(width, width)
+        for array in (near, far)
+        for part in range(2)
     ]
-    down_start = (4 + fold) * own_rows
-    down_full = gathered[:, down_start : down_start + feed_rows].reshape(feed_width, width)
-    line = gathered[:, down_start + feed_rows :].reshape(device_count, -1)
-    lines = cut_line(line, [vector.shape[0] for vector in vectors])
-    lines = [part.reshape(-1) for part in lines]
-    attention_full = tuple(square[:4]) + tuple(lines[:5])
-    feed_full = (
-        jnp.concatenate(square[4:], axis=1),
-        down_full,
-        lines[8],
-        lines[5],
-        lines[6],
-        lines[7],
-    )
+    line = near[:, 2 * own_rows :].reshape(device_count, -1)
+    lines = cut_line(line, [own_rows] * 5)
+    attention_full = tuple(square) + tuple(part.reshape(-1) for part in lines)
 
     output, stored = forward_pass(tokens, lengths, attention_full, feed_full)
     input_grad, attention_terms, feed_terms = backward_pass(
@@ -326,38 +394,48 @@
         return vector.reshape(device_count, -1)
 
     up_term, down_term, up_bias_term, down_bias_term, gain_term, shift_term = feed_terms
-    feed_packed = pack_rows(
-        up_pieces(up_term, device_count) + [to_blocks(down_term)],
+    down_packed = pack_rows(
+        [to_blocks(down_term)],
         [to_lines(part) for part in (up_bias_term, down_bias_term, gain_term, shift_term)],
         width,
         jnp.bfloat16,
     )
-    feed_owned = lax.psum_scatter(
-        feed_packed.reshape(-1, width), "fsdp", scatter_dimension=0, tiled=True
-    )
-    attention_packed = pack_rows(
-        [to_blocks(part) for part in attention_terms[:4]],
-        [to_lines(part) for part in attention_terms[4:]],
-        width,
-        jnp.bfloat16,
-    )
-    attention_owned = lax.psum_scatter(
-        attention_packed.reshape(-1, width), "fsdp", scatter_dimension=0, tiled=True
-    )
-    feed_owned = feed_owned.astype(jnp.float32)
-    attention_owned = attention_owned.astype(jnp.float32)
+    down_sum = scatter_sum(down_packed, sizes, X_FIRST)
+    up_sum = scatter_sum(
+        jnp.concatenate(
+            [part.astype(jnp.bfloat16) for part in up_pieces(up_term, device_count)], axis=1
+        ),
+        sizes,
+        Y_FIRST,
+    )
+    query_term, key_term, value_term, out_term = [to_blocks(part) for part in attention_terms[:4]]
+    far_sum = scatter_sum(
+        jnp.concatenate([value_term, out_term], axis=1).astype(jnp.bfloat16), sizes, X_FIRST
+    )
+    near_sum = scatter_sum(
+        pack_rows(
+            [query_term, key_term],
+            [to_lines(part) for part in attention_terms[4:]],
+            width,
+            jnp.bfloat16,
+        ),
+        sizes,
+        Y_FIRST,
+    )
     up_owned = jnp.concatenate(
-        [feed_owned[part * own_rows : (part + 1) * own_rows] for part in range(fold)], axis=1
-    )
-    down_owned = feed_owned[fold * own_rows : fold * own_rows + feed_rows]
-    feed_line = feed_owned[fold * own_rows + feed_rows :].reshape(1, -1)
+        [up_sum[part * own_rows : (part + 1) * own_rows] for part in range(fold)], axis=1
+    )
+    down_owned = down_sum[:feed_rows]
+    feed_line = down_sum[feed_rows:].reshape(1, -1)
     feed_vectors = [
         part[0] for part in cut_line(feed_line, [feed_rows, own_rows, own_rows, own_rows])
     ]
     squares_owned = [
-        attention_owned[part * own_rows : (part + 1) * own_rows] for part in range(4)
+        array[part * own_rows : (part + 1) * own_rows]
+        for array in (near_sum, far_sum)
+        for part in range(2)
     ]
-    attention_line = attention_owned[4 * own_rows :].reshape(1, -1)
+    attention_line = near_sum[2 * own_rows :].reshape(1, -1)
     attention_vectors = [part[0] for part in cut_line(attention_line, [own_rows] * 5)]
     return (
         output,

time: 671 us -> 509 us (0.76)
  waiting for transfers between devices: 319 us -> 116 us
  starting transfers between devices: 0.12 us -> 49.6 us
  matrix products: 197 us -> 169 us
  other arithmetic: 44.1 us -> 58.6 us
  local copies, waits for them, and re-layouts: 85.9 us -> 96.4 us
    reduce_scatter x2 -> x0, waiting for transfers between devices: 215 us -> none  [the longest x1 142 us: shards(): lax.psum_scatter(feed_packed.reshape(-1, width), 'fsdp', scatter_dimensio...]
    ppermute x0 -> x36, waiting for transfers between devices: none -> 116 us  [the longest x24 81.2 us: scatter_sum(): lax.ppermute(part, 'fsdp', shifted_pairs(sizes, axis, shift))]
    all_gather x1, waiting for transfers between devices: 104 us -> 0.02 us  [shards(): gathered = lax.all_gather(feed_packed[0], 'fsdp', axis=0, tiled=False)]
    ppermute x0 -> x36, starting transfers between devices: none -> 49.5 us  [the longest x24 27.8 us: scatter_sum(): lax.ppermute(part, 'fsdp', shifted_pairs(sizes, axis, shift))]
    dot_general x6, matrix products: 61.1 us -> 32.3 us  [times_plain(): return jnp.dot(left_side, right_side, preferred_element_type=jnp.float32)]
    convert_element_type x2 -> x13, other arithmetic: 1.95 us -> 11.3 us  [the longest x12 11.2 us: scatter_sum(): held = held.astype(jnp.bfloat16)]
    dot_general x6, matrix products: 39.2 us -> 31.3 us  [times_back(): lax.dot_general(left_side, right_side, (((1,), (1,)), ((), ())), preferre...]
    dot_general x6, matrix products: 23.8 us -> 30.5 us  [times_across(): lax.dot_general(left_side, right_side, (((0,), (0,)), ((), ())), preferre...]
  transfers between devices with their start and end apart: 3 -> 37, of which waited for: 3 -> 18; matrix products, arithmetic and copies ran while one was open for 7% -> 25% of each run, Pallas kernels for 0% -> 0%
where the time goes in v2:
time: 509 us; the launch traced here: 505 us
  matrix products  169 us (33%)
  waiting for transfers between devices  116 us (23%)
  local copies, waits for them, and re-layouts  96.4 us (19%)
  other arithmetic  58.6 us (12%)
  starting transfers between devices  49.6 us (10%)
  between operations  15.9 us (3%)
    ppermute x24, waiting for transfers between devices, scatter_sum(): lax.ppermute(part, 'fsdp', shifted_pairs(sizes, axis, shift))  81.2 us
    unnamed x120, local copies, waits for them, and re-layouts  34.7 us
    ppermute x12, waiting for transfers between devices, gather_blocks(): part = lax.ppermute(held, 'fsdp', shifted_pairs(sizes, axis, shift))  34.3 us
    dot_general x6, matrix products, times_plain(): return jnp.dot(left_side, right_side, preferred_element_type=jnp.float32)  32.3 us
    dot_general x6, matrix products, times_back(): lax.dot_general(left_side, right_side, (((1,), (1,)), ((), ())), preferre...  31.3 us
    dot_general x6, matrix products, times_across(): lax.dot_general(left_side, right_side, (((0,), (0,)), ((), ())), preferre...  30.5 us
    ppermute x24, starting transfers between devices, scatter_sum(): lax.ppermute(part, 'fsdp', shifted_pairs(sizes, axis, shift))  27.8 us
    convert_element_type x1, other arithmetic, backward_pass(): grad_scores = (probs * (grad_probs - row_delta)).astype(jnp.bfloat16)  21.8 us
  transfers between devices with their start and end apart: 37, of which 18 were waited for; matrix products, arithmetic and copies ran while one was open for 25% of the time, Pallas kernels for 0%

profile of v2, /device:TPU:0, one launch (start us, length us, event | category | flops | bytes accessed | tf_op | source)
XLA Modules:
  0.0 505.1 jit_solution(3278059606780865889)
XLA Ops:
  14.4 5.0 collective-permute-start.2
  26.4 6.4 %collective-permute-start.6 = (bf16[64,768]{1,0:T(8,128)(2,1)S(1)}, bf16[64,768]{1,0:T(8,128)(2,1)S(1)}, u32[]{:S(2)}, u32[]{:S(2)}) collective-permute-start(bf16[64,768]{1,0:T(8,128)(2,1)S(1)} %get-tuple-element.129), channel_id=1, source_target_pairs={{0,8},{1,9},{2,10},{3,11},{4,12},{5,13},{6,14},{7,15},{8,16},{9,17... | collective-permute-start | bytes 294920 | tf_op jit(solution)/shard_map/ppermute | solution.py:278
  35.2 6.4 %collective-permute-done.7 = bf16[64,768]{1,0:T(8,128)(2,1)S(1)} collective-permute-done((bf16[64,768]{1,0:T(8,128)(2,1)S(1)}, bf16[64,768]{1,0:T(8,128)(2,1)S(1)}, u32[]{:S(2)}, u32[]{:S(2)}) %collective-permute-start.7) | collective-permute-done | bytes 98336 | tf_op jit(solution)/shard_map/ppermute | solution.py:278
  43.9 13.7 %collective-permute-done.9 = bf16[4,64,768]{2,1,0:T(8,128)(2,1)S(1)} collective-permute-done((bf16[4,64,768]{2,1,0:T(8,128)(2,1)S(1)}, bf16[4,64,768]{2,1,0:T(8,128)(2,1)S(1)}, u32[]{:S(2)}, u32[]{:S(2)}) %collective-permute-start.9) | collective-permute-done | bytes 393248 | tf_op jit(solution)/shard_map/ppermute | solution.py:278
  61.4 6.4 %collective-permute-done.4 = bf16[4,2,48,768]{3,2,1,0:T(8,128)(2,1)S(1)} collective-permute-done((bf16[4,2,48,768]{3,2,1,0:T(8,128)(2,1)S(1)}, bf16[4,2,48,768]{3,2,1,0:T(8,128)(2,1)S(1)}, u32[]{:S(2)}, u32[]{:S(2)}) %collective-permute-start.4) | collective-permute-done | bytes 589856 | tf_op jit(solution)/shard_map/ppermute | solution.py:278
  68.7 7.0 %collective-permute-done.10 = bf16[4,2,64,768]{3,2,1,0:T(8,128)(2,1)S(1)} collective-permute-done((bf16[4,2,64,768]{3,2,1,0:T(8,128)(2,1)S(1)}, bf16[4,2,64,768]{3,2,1,0:T(8,128)(2,1)S(1)}, u32[]{:S(2)}, u32[]{:S(2)}) %collective-permute-start.10) | collective-permute-done | bytes 786464 | tf_op jit(solution)/shard_map/ppermute | solution.py:278
  90.5 4.1 fusion.38
  105.2 4.0 reshape.416
  115.9 13.3 %fusion.6 = (f32[2,12,512]{2,1,0:T(8,128)S(1)}, f32[2,12,512,512]{2,3,1,0:T(8,128)}) fusion(pred[2,512]{1,0:T(4,128)(4,1)S(1)} %get-tuple-element.142, bf16[2,512,12,64]{1,0,3,2:T(2,128)(2,1)S(1)} %reshape.418, bf16[2,512,12,64]{1,0,3,2:T(2,128)(2,1)} %reshape.416), kind=kOutput, calls=%fused_computation.14 | convolution fusion | flops 824168448 | bytes 28361728 | tf_op jit(solution)/shard_map/sqhd,skhd->shqk/dot_general | solution.py:53
  129.1 11.6 %fusion = f32[2,12,512]{2,1,0:T(8,128)S(1)} fusion(f32[2,12,512]{2,1,0:T(8,128)S(1)} %get-tuple-element.143, f32[2,12,512,512]{2,3,1,0:T(8,128)} %get-tuple-element.144, pred[2,512]{1,0:T(4,128)(4,1)S(1)} %get-tuple-element.142), kind=kLoop, calls=%fused_computation.6 | loop fusion | flops 25153536 | bytes 25265152 | tf_op jit(solution)/shard_map/reduce_sum | solution.py:87
  140.8 11.4 %fusion.40 = bf16[2,512,12,64]{1,3,2,0:T(8,128)(2,1)S(1)} fusion(f32[2,12,512]{2,1,0:T(8,128)S(1)} %fusion, f32[2,12,512]{2,1,0:T(8,128)S(1)} %get-tuple-element.143, f32[2,12,512,512]{2,3,1,0:T(8,128)} %get-tuple-element.144, pred[2,512]{1,0:T(4,128)(4,1)S(1)} %get-tuple-element.142, bf16[2,512,12,64]{1,0,3,2:T(2,128)(2,1)S(1)} %copy-done.13), kind=kOutput, calls=%fused_computation.97 | convolution fusion | flops 837550080 | bytes 28410880 | tf_op jit(solution)/shard_map/shqk,skhd->sqhd/dot_general | solution.py:90
  163.8 12.4 %multiply_convert_fusion.1 = (bf16[1024,3072]{1,0:T(8,128)(2,1)}, f32[1024,3072]{1,0:T(8,128)}) fusion(f32[3072]{0:T(1024)S(1)} %reshape.439, bf16[768,768]{1,0:T(8,128)(2,1)S(1)} %bitcast.364, bf16[768,768]{1,0:T(8,128)(2,1)S(1)} %bitcast.366, bf16[768,768]{1,0:T(8,128)(2,1)S(1)} %bitcast.368, bf16[768,768]{1,0:T(8,128)(2,1)S(1)} %bitcast.362, ...), kind=kOutput, calls=%fused_computation.11 | convolution fusion | flops 4873519104 | bytes 26765312 | tf_op jit(solution)/shard_map/dot_general | solution.py:24
  178.8 7.7 %fusion.97 = (f32[1024]{0:T(1024)S(1)}, f32[1024,768]{0,1:T(8,128)S(1)}) fusion(f32[768]{0:T(1024)S(1)} %reshape.440, bf16[1024,3072]{1,0:T(8,128)(2,1)} %get-tuple-element.147, bf16[3072,768]{1,0:T(8,128)(2,1)S(1)} %bitcast.346, f32[768]{0:T(1024)S(1)} %reshape.438, f32[768]{0:T(1024)S(1)} %reshape.437, f32[1024]{0:T(1024)S(1)} %fusion.75, ...), kind=kOutput, calls=%fused_computation.248 | convolution fusion | flops 4837342208 | bytes 17323008 | tf_op jit(solution)/shard_map/dot_general | solution.py:24
  191.9 9.9 %convolution_convert_fusion = bf16[3072,768]{1,0:T(8,128)(2,1)} fusion(bf16[1024,3072]{1,0:T(8,128)(2,1)} %get-tuple-element.147, bf16[1024,768]{0,1:T(8,128)(2,1)S(1)} %get-tuple-element.77), kind=kOutput, calls=%fused_computation.21 | convolution fusion | flops 4834197504 | bytes 12582912 | tf_op jit(solution)/shard_map/dot_general | solution.py:28
  201.8 13.4 %fusion.100 = (bf16[3072]{0:T(1024)(128)(2,1)S(1)}, bf16[1024,3072]{1,0:T(8,128)(2,1)}) fusion(f32[1024,3072]{1,0:T(8,128)S(1)} %bitcast.400, f32[3072]{0:T(1024)S(1)} %reshape.439, bf16[1024,768]{0,1:T(8,128)(2,1)S(1)} %get-tuple-element.77, bf16[3072,768]{1,0:T(8,128)(2,1)S(1)} %bitcast.347), kind=kOutput, calls=%fused_computation.251 | convolution fusion | flops 4875875328 | bytes 25184256 | tf_op jit(solution)/shard_map/dot_general | solution.py:34
  215.2 9.9 %multiply_reduce_fusion.2 = (bf16[768]{0:T(1024)(128)(2,1)S(1)}, f32[1024]{0:T(1024)S(1)}, bf16[768]{0:T(1024)(128)(2,1)S(1)}, f32[1024,768]{0,1:T(8,128)S(1)}) fusion(f32[1024,768]{0,1:T(8,128)S(1)} %copy-done.4, f32[1024]{0:T(1024)S(1)} %fusion.75, f32[1024]{0:T(1024)S(1)} %broadcast_multiply_fusion.1, f32[768]{0:T(1024)S(1)} %reshape.437, ...), kind=kOutput, calls=%fused_computation.33 | convolution fusion | flops 4864865280 | bytes 22062080 | tf_op jit(solution)/shard_map/dot_general | solution.py:34
  225.1 9.8 %convolution_convert_fusion.1 = bf16[768,3072]{1,0:T(8,128)(2,1)} fusion(bf16[1024,3072]{1,0:T(8,128)(2,1)} %get-tuple-element.159, f32[1024,768]{0,1:T(8,128)S(1)} %copy-done.4, f32[768]{0:T(1024)S(1)} %reshape.438, f32[768]{0:T(1024)S(1)} %reshape.437, f32[1024]{0:T(1024)S(1)} %fusion.75, f32[1024]{0:T(1024)S(1)} %broadcast_multiply_fusion.1), kind=kOutput, calls=%fused_computation.22 | convolution fusion | flops 4838129664 | bytes 14170112 | tf_op jit(solution)/shard_map/dot_general | solution.py:28
  242.5 3.9 reshape.431
  246.3 12.9 %fusion.99 = (bf16[12,64]{1,0:T(8,128)(2,1)S(1)}, bf16[2,512,12,64]{1,3,2,0:T(8,128)(2,1)}) fusion(f32[2,12,512]{2,1,0:T(8,128)S(1)} %log_add_fusion, f32[2,12,512,512]{2,3,1,0:T(8,128)} %get-tuple-element.144, pred[2,512]{1,0:T(4,128)(4,1)S(1)} %get-tuple-element.142, bf16[2,512,12,64]{1,0,3,2:T(2,128)(2,1)} %reshape.431), kind=kOutput, calls=%fused_computation.250 | convolution fusion | flops 832044288 | bytes 28363264 | tf_op jit(solution)/shard_map/shqk,sqhd->skhd/dot_general | solution.py:177
  259.2 19.7 %multiply_reduce_fusion = (f32[2,12,512]{2,1,0:T(8,128)S(1)}, f32[2,12,512,512]{2,3,1,0:T(8,128)}) fusion(f32[2,12,512]{2,1,0:T(8,128)S(1)} %log_add_fusion, f32[2,12,512,512]{2,3,1,0:T(8,128)} %get-tuple-element.144, pred[2,512]{1,0:T(4,128)(4,1)S(1)} %get-tuple-element.142, bf16[2,512,12,64]{1,0,3,2:T(2,128)(2,1)} %reshape.414, ...), kind=kOutput, calls=%fused_computation.1 | convolution fusion | flops 836751360 | bytes 53576704 | tf_op jit(solution)/shard_map/sqhd,skhd->shqk/dot_general | solution.py:174
  278.9 21.8 %multiply_convert_fusion = bf16[2,12,512,512]{2,3,1,0:T(8,128)(2,1)} fusion(f32[2,12,512,512]{2,3,1,0:T(8,128)} %get-tuple-element.153, f32[2,12,512]{2,1,0:T(8,128)S(1)} %get-tuple-element.152, f32[2,12,512]{2,1,0:T(8,128)S(1)} %log_add_fusion, f32[2,12,512,512]{2,3,1,0:T(8,128)} %get-tuple-element.144, pred[2,512]{1,0:T(4,128)(4,1)S(1)} %get-tuple-element.142), kind=kLoop, calls=%fused_computation | loop fusion | flops 37748736 | bytes 63013888 | tf_op jit(solution)/shard_map/convert_element_type | solution.py:185
  300.8 9.7 %fusion.36 = bf16[2,512,12,64]{1,3,2,0:T(8,128)(2,1)} fusion(bf16[2,12,512,512]{2,3,1,0:T(8,128)(2,1)} %multiply_convert_fusion, bf16[2,512,12,64]{1,0,3,2:T(2,128)(2,1)S(1)} %copy-done.2), kind=kOutput, calls=%fused_computation.93 | convolution fusion | flops 806879232 | bytes 15728640 | tf_op jit(solution)/shard_map/shqk,sqhd->skhd/dot_general | solution.py:191
  310.5 7.9 %fusion.98 = (bf16[12,64]{1,0:T(8,128)(2,1)S(1)}, bf16[2,512,12,64]{1,3,2,0:T(8,128)(2,1)}) fusion(bf16[2,12,512,512]{2,3,1,0:T(8,128)(2,1)} %multiply_convert_fusion, bf16[2,512,12,64]{1,0,3,2:T(2,128)(2,1)S(1)} %copy-done.1), kind=kOutput, calls=%fused_computation.249 | convolution fusion | flops 807664896 | bytes 15730176 | tf_op jit(solution)/shard_map/shqk,skhd->sqhd/dot_general | solution.py:187
  318.7 4.6 fusion.90
  324.8 4.4 fusion.29
  374.7 8.8 %collective-permute-done.19 = bf16[4,2,48,768]{3,2,1,0:T(8,128)(2,1)} collective-permute-done((bf16[4,2,48,768]{3,2,1,0:T(8,128)(2,1)}, bf16[4,2,48,768]{3,2,1,0:T(8,128)(2,1)}, u32[]{:S(2)}, u32[]{:S(2)}) %collective-permute-start.19) | collective-permute-done | bytes 589856 | tf_op jit(solution)/shard_map/ppermute | solution.py:258
  388.2 5.1 %collective-permute-done.20 = bf16[4,48,768]{2,1,0:T(8,128)(2,1)S(1)} collective-permute-done((bf16[4,48,768]{2,1,0:T(8,128)(2,1)S(1)}, bf16[4,48,768]{2,1,0:T(8,128)(2,1)S(1)}, u32[]{:S(2)}, u32[]{:S(2)}) %collective-permute-start.20) | collective-permute-done | bytes 294944 | tf_op jit(solution)/shard_map/ppermute | solution.py:258
  407.6 12.8 %collective-permute-done.13 = bf16[4,2,64,768]{3,2,0,1:T(8,128)(2,1)S(1)} collective-permute-done((bf16[4,2,64,768]{3,2,0,1:T(8,128)(2,1)S(1)}, bf16[4,2,64,768]{3,2,0,1:T(8,128)(2,1)S(1)}, u32[]{:S(2)}, u32[]{:S(2)}) %collective-permute-start.13) | collective-permute-done | bytes 786464 | tf_op jit(solution)/shard_map/ppermute | solution.py:258
  425.5 7.3 %collective-permute-done.14 = bf16[4,64,768]{2,1,0:T(8,128)(2,1)S(1)} collective-permute-done((bf16[4,64,768]{2,1,0:T(8,128)(2,1)S(1)}, bf16[4,64,768]{2,1,0:T(8,128)(2,1)S(1)}, u32[]{:S(2)}, u32[]{:S(2)}) %collective-permute-start.14) | collective-permute-done | bytes 393248 | tf_op jit(solution)/shard_map/ppermute | solution.py:258
  444.3 22.0 %collective-permute-done.26 = bf16[4,96,768]{2,1,0:T(8,128)(2,1)S(1)} collective-permute-done((bf16[4,96,768]{2,1,0:T(8,128)(2,1)S(1)}, bf16[4,96,768]{2,1,0:T(8,128)(2,1)S(1)}, u32[]{:S(2)}, u32[]{:S(2)}) %collective-permute-start.26) | collective-permute-done | bytes 589856 | tf_op jit(solution)/shard_map/ppermute | solution.py:258
  473.6 9.3 %collective-permute-done.28 = bf16[96,768]{1,0:T(8,128)(2,1)S(1)} collective-permute-done((bf16[96,768]{1,0:T(8,128)(2,1)S(1)}, bf16[96,768]{1,0:T(8,128)(2,1)S(1)}, u32[]{:S(2)}, u32[]{:S(2)}) %collective-permute-start.28) | collective-permute-done | bytes 147488 | tf_op jit(solution)/shard_map/ppermute | solution.py:258
  490.8 5.1 %collective-permute-done.34 = bf16[112,768]{1,0:T(8,128)(2,1)S(1)} collective-permute-done((bf16[112,768]{1,0:T(8,128)(2,1)S(1)}, bf16[112,768]{1,0:T(8,128)(2,1)S(1)}, u32[]{:S(2)}, u32[]{:S(2)}) %collective-permute-start.34) | collective-permute-done | bytes 172064 | tf_op jit(solution)/shard_map/ppermute | solution.py:258
  (323 shorter events, 181.4 us)
Async XLA Ops:
  7.2 150.9 %all-gather.2.cloned.1.call-start = ((), (), s32[]{:S(2)}) async-start(), calls=%async_computation | async-start | bytes 10543104 | tf_op jit(solution)/shard_map/all_gather | solution.py:351
  14.4 18.5 %collective-permute-start.2 = (bf16[48,768]{1,0:T(8,128)(2,1)S(1)}, bf16[48,768]{1,0:T(8,128)(2,1)S(1)}, u32[]{:S(2)}, u32[]{:S(2)}) collective-permute-start(bf16[48,768]{1,0:T(8,128)(2,1)S(1)} %constant_dynamic-update-slice_fusion), channel_id=1, source_target_pairs={{0,24},{1,25},{2,26},{3,27},{4,28},{5,29},{6,30},{7,31},{8,0},{9,1... | collective-permute-start | bytes 221192 | tf_op jit(solution)/shard_map/ppermute | solution.py:278
  19.4 13.4 %collective-permute-start.1 = (bf16[48,768]{1,0:T(8,128)(2,1)S(1)}, bf16[48,768]{1,0:T(8,128)(2,1)S(1)}, u32[]{:S(2)}, u32[]{:S(2)}) collective-permute-start(bf16[48,768]{1,0:T(8,128)(2,1)S(1)} %constant_dynamic-update-slice_fusion), channel_id=1, source_target_pairs={{0,16},{1,17},{2,18},{3,19},{4,20},{5,21},{6,22},{7,23},{8,24},{9,... | collective-permute-start | bytes 221192 | tf_op jit(solution)/shard_map/ppermute | solution.py:278
  22.2 19.4 %collective-permute-start.8 = (bf16[64,768]{1,0:T(8,128)(2,1)S(1)}, bf16[64,768]{1,0:T(8,128)(2,1)S(1)}, u32[]{:S(2)}, u32[]{:S(2)}) collective-permute-start(bf16[64,768]{1,0:T(8,128)(2,1)S(1)} %get-tuple-element.129), channel_id=1, source_target_pairs={{0,24},{1,25},{2,26},{3,27},{4,28},{5,29},{6,30},{7,31},{8,0},{9,1... | collective-permute-start | bytes 294920 | tf_op jit(solution)/shard_map/ppermute | solution.py:278
  25.1 16.5 %collective-permute-start.7 = (bf16[64,768]{1,0:T(8,128)(2,1)S(1)}, bf16[64,768]{1,0:T(8,128)(2,1)S(1)}, u32[]{:S(2)}, u32[]{:S(2)}) collective-permute-start(bf16[64,768]{1,0:T(8,128)(2,1)S(1)} %get-tuple-element.129), channel_id=1, source_target_pairs={{0,16},{1,17},{2,18},{3,19},{4,20},{5,21},{6,22},{7,23},{8,24},{9,... | collective-permute-start | bytes 294920 | tf_op jit(solution)/shard_map/ppermute | solution.py:278
  26.4 8.7 %collective-permute-start.6 = (bf16[64,768]{1,0:T(8,128)(2,1)S(1)}, bf16[64,768]{1,0:T(8,128)(2,1)S(1)}, u32[]{:S(2)}, u32[]{:S(2)}) collective-permute-start(bf16[64,768]{1,0:T(8,128)(2,1)S(1)} %get-tuple-element.129), channel_id=1, source_target_pairs={{0,8},{1,9},{2,10},{3,11},{4,12},{5,13},{6,14},{7,15},{8,16},{9,17... | collective-permute-start | bytes 294920 | tf_op jit(solution)/shard_map/ppermute | solution.py:278
  32.9 10.3 %collective-permute-start.3 = (bf16[4,48,768]{2,1,0:T(8,128)(2,1)S(1)}, bf16[4,48,768]{2,1,0:T(8,128)(2,1)S(1)}, u32[]{:S(2)}, u32[]{:S(2)}) collective-permute-start(bf16[4,48,768]{2,1,0:T(8,128)(2,1)S(1)} %bitcast_dynamic-update-slice_fusion.16), channel_id=1, source_target_pairs={{0,2},{1,3},{2,0},{3,1},{4,6},{5,7},{6,4},{7,5},{8,10},{9,11},{10,... | collective-permute-start | bytes 884744 | tf_op jit(solution)/shard_map/ppermute | solution.py:278
  41.6 16.0 %collective-permute-start.9 = (bf16[4,64,768]{2,1,0:T(8,128)(2,1)S(1)}, bf16[4,64,768]{2,1,0:T(8,128)(2,1)S(1)}, u32[]{:S(2)}, u32[]{:S(2)}) collective-permute-start(bf16[4,64,768]{2,1,0:T(8,128)(2,1)S(1)} %bitcast_dynamic-update-slice_fusion.13), channel_id=1, source_target_pairs={{0,4},{1,5},{2,6},{3,7},{4,0},{5,1},{6,2},{7,3},{8,12},{9,13},{10,... | collective-permute-start | bytes 1179656 | tf_op jit(solution)/shard_map/ppermute | solution.py:278
  43.2 24.6 %collective-permute-start.4 = (bf16[4,2,48,768]{3,2,1,0:T(8,128)(2,1)S(1)}, bf16[4,2,48,768]{3,2,1,0:T(8,128)(2,1)S(1)}, u32[]{:S(2)}, u32[]{:S(2)}) collective-permute-start(bf16[4,2,48,768]{3,2,1,0:T(8,128)(2,1)S(1)} %bitcast_dynamic-update-slice_fusion.11), channel_id=1, source_target_pairs={{0,4},{1,5},{2,6},{3,7},{4,0},{5,1},{6,2},{7,3},{8,12},{9,13},{10,... | collective-permute-start | bytes 1769480 | tf_op jit(solution)/shard_map/ppermute | solution.py:278
  57.7 18.1 %collective-permute-start.10 = (bf16[4,2,64,768]{3,2,1,0:T(8,128)(2,1)S(1)}, bf16[4,2,64,768]{3,2,1,0:T(8,128)(2,1)S(1)}, u32[]{:S(2)}, u32[]{:S(2)}) collective-permute-start(bf16[4,2,64,768]{3,2,1,0:T(8,128)(2,1)S(1)} %bitcast_dynamic-update-slice_fusion.9), channel_id=1, source_target_pairs={{0,2},{1,3},{2,0},{3,1},{4,6},{5,7},{6,4},{7,5},{8,10},{9,11},{10,... | collective-permute-start | bytes 2359304 | tf_op jit(solution)/shard_map/ppermute | solution.py:278
  68.7 14.5 %collective-permute-start.5 = (bf16[4,2,2,48,768]{4,3,2,1,0:T(8,128)(2,1)}, bf16[4,2,2,48,768]{4,3,2,1,0:T(8,128)(2,1)}, u32[]{:S(2)}, u32[]{:S(2)}) collective-permute-start(bf16[4,2,2,48,768]{4,3,2,1,0:T(8,128)(2,1)} %bitcast_dynamic-update-slice_fusion.7), channel_id=1, source_target_pairs={{0,1},{1,0},{2,3},{3,2},{4,5},{5,4},{6,7},{7,6},{8,9},{9,8},{10,11... | collective-permute-start | bytes 3538952 | tf_op jit(solution)/shard_map/ppermute | solution.py:278
  75.8 10.5 %collective-permute-start.11 = (bf16[4,2,2,64,768]{4,3,2,1,0:T(8,128)(2,1)S(1)}, bf16[4,2,2,64,768]{4,3,2,1,0:T(8,128)(2,1)}, u32[]{:S(2)}, u32[]{:S(2)}) collective-permute-start(bf16[4,2,2,64,768]{4,3,2,1,0:T(8,128)(2,1)S(1)} %bitcast_dynamic-update-slice_fusion.5), channel_id=1, source_target_pairs={{0,1},{1,0},{2,3},{3,2},{4,5},{5,4},{6,7},{7,6},{8,9},{9,8},{10,11... | collective-permute-start | bytes 4718600 | tf_op jit(solution)/shard_map/ppermute | solution.py:278
  339.9 23.7 %collective-permute-start.18 = (bf16[4,2,2,48,768]{4,3,2,1,0:T(8,128)(2,1)}, bf16[4,2,2,48,768]{4,3,2,1,0:T(8,128)(2,1)}, u32[]{:S(2)}, u32[]{:S(2)}) collective-permute-start(bf16[4,2,2,48,768]{4,3,2,1,0:T(8,128)(2,1)} %fusion.53), channel_id=1, source_target_pairs={{0,1},{1,0},{2,3},{3,2},{4,5},{5,4},{6,7},{7,6},{8,9},{9,8},{10,11... | collective-permute-start | bytes 3538952 | tf_op jit(solution)/shard_map/ppermute | solution.py:258
  341.6 62.0 %collective-permute-start.24 = (bf16[4,2,2,96,768]{4,3,0,2,1:T(8,128)(2,1)}, bf16[4,2,2,96,768]{4,3,0,2,1:T(8,128)(2,1)}, u32[]{:S(2)}, u32[]{:S(2)}) collective-permute-start(bf16[4,2,2,96,768]{4,3,0,2,1:T(8,128)(2,1)} %bitcast.326), channel_id=1, source_target_pairs={{0,1},{1,0},{2,3},{3,2},{4,5},{5,4},{6,7},{7,6},{8,9},{9,8},{10,11... | collective-permute-start | bytes 7077896 | tf_op jit(solution)/shard_map/ppermute | solution.py:258
  355.7 30.5 %collective-permute-start.12 = (bf16[4,2,2,64,768]{4,3,0,2,1:T(8,128)(2,1)}, bf16[4,2,2,64,768]{4,3,0,2,1:T(8,128)(2,1)}, u32[]{:S(2)}, u32[]{:S(2)}) collective-permute-start(bf16[4,2,2,64,768]{4,3,0,2,1:T(8,128)(2,1)} %bitcast.327), channel_id=1, source_target_pairs={{0,1},{1,0},{2,3},{3,2},{4,5},{5,4},{6,7},{7,6},{8,9},{9,8},{10,11... | collective-permute-start | bytes 4718600 | tf_op jit(solution)/shard_map/ppermute | solution.py:258
  363.3 58.3 %collective-permute-start.30 = (bf16[4,2,2,112,768]{4,3,0,1,2:T(8,128)(2,1)}, bf16[4,2,2,112,768]{4,3,0,1,2:T(8,128)(2,1)}, u32[]{:S(2)}, u32[]{:S(2)}) collective-permute-start(bf16[4,2,2,112,768]{4,3,0,1,2:T(8,128)(2,1)} %bitcast.325), channel_id=1, source_target_pairs={{0,1},{1,0},{2,3},{3,2},{4,5},{5,4},{6,7},{7,6},{8,9},{9,8},{10,11... | collective-permute-start | bytes 8257544 | tf_op jit(solution)/shard_map/ppermute | solution.py:258
  367.6 15.8 %collective-permute-start.19 = (bf16[4,2,48,768]{3,2,1,0:T(8,128)(2,1)}, bf16[4,2,48,768]{3,2,1,0:T(8,128)(2,1)}, u32[]{:S(2)}, u32[]{:S(2)}) collective-permute-start(bf16[4,2,48,768]{3,2,1,0:T(8,128)(2,1)} %dynamic-slice_bitcast_fusion.5), channel_id=1, source_target_pairs={{0,2},{1,3},{2,0},{3,1},{4,6},{5,7},{6,4},{7,5},{8,10},{9,11},{10,... | collective-permute-start | bytes 1769480 | tf_op jit(solution)/shard_map/ppermute | solution.py:258
  384.9 8.4 %collective-permute-start.20 = (bf16[4,48,768]{2,1,0:T(8,128)(2,1)S(1)}, bf16[4,48,768]{2,1,0:T(8,128)(2,1)S(1)}, u32[]{:S(2)}, u32[]{:S(2)}) collective-permute-start(bf16[4,48,768]{2,1,0:T(8,128)(2,1)S(1)} %dynamic-slice_bitcast_fusion.7), channel_id=1, source_target_pairs={{0,4},{1,5},{2,6},{3,7},{4,0},{5,1},{6,2},{7,3},{8,12},{9,13},{10,... | collective-permute-start | bytes 884744 | tf_op jit(solution)/shard_map/ppermute | solution.py:258
  399.9 20.5 %collective-permute-start.13 = (bf16[4,2,64,768]{3,2,0,1:T(8,128)(2,1)S(1)}, bf16[4,2,64,768]{3,2,0,1:T(8,128)(2,1)S(1)}, u32[]{:S(2)}, u32[]{:S(2)}) collective-permute-start(bf16[4,2,64,768]{3,2,0,1:T(8,128)(2,1)S(1)} %dynamic-slice_bitcast_fusion.2), channel_id=1, source_target_pairs={{0,4},{1,5},{2,6},{3,7},{4,0},{5,1},{6,2},{7,3},{8,12},{9,13},{10,... | collective-permute-start | bytes 2359304 | tf_op jit(solution)/shard_map/ppermute | solution.py:258
  406.1 35.7 %collective-permute-start.25 = (bf16[4,2,96,768]{3,2,0,1:T(8,128)(2,1)S(1)}, bf16[4,2,96,768]{3,2,0,1:T(8,128)(2,1)S(1)}, u32[]{:S(2)}, u32[]{:S(2)}) collective-permute-start(bf16[4,2,96,768]{3,2,0,1:T(8,128)(2,1)S(1)} %dynamic-slice_bitcast_fusion.1), channel_id=1, source_target_pairs={{0,4},{1,5},{2,6},{3,7},{4,0},{5,1},{6,2},{7,3},{8,12},{9,13},{10,... | collective-permute-start | bytes 3538952 | tf_op jit(solution)/shard_map/ppermute | solution.py:258
  420.6 12.1 %collective-permute-start.14 = (bf16[4,64,768]{2,1,0:T(8,128)(2,1)S(1)}, bf16[4,64,768]{2,1,0:T(8,128)(2,1)S(1)}, u32[]{:S(2)}, u32[]{:S(2)}) collective-permute-start(bf16[4,64,768]{2,1,0:T(8,128)(2,1)S(1)} %dynamic-slice_bitcast_fusion.6), channel_id=1, source_target_pairs={{0,2},{1,3},{2,0},{3,1},{4,6},{5,7},{6,4},{7,5},{8,10},{9,11},{10,... | collective-permute-start | bytes 1179656 | tf_op jit(solution)/shard_map/ppermute | solution.py:258
  424.4 46.0 %collective-permute-start.31 = (bf16[4,2,112,768]{3,2,0,1:T(8,128)(2,1)S(1)}, bf16[4,2,112,768]{3,2,0,1:T(8,128)(2,1)S(1)}, u32[]{:S(2)}, u32[]{:S(2)}) collective-permute-start(bf16[4,2,112,768]{3,2,0,1:T(8,128)(2,1)S(1)} %dynamic-slice_bitcast_fusion), channel_id=1, source_target_pairs={{0,2},{1,3},{2,0},{3,1},{4,6},{5,7},{6,4},{7,5},{8,10},{9,11},{10,... | collective-permute-start | bytes 4128776 | tf_op jit(solution)/shard_map/ppermute | solution.py:258
  432.9 10.6 %collective-permute-start.15 = (bf16[64,768]{1,0:T(8,128)(2,1)S(1)}, bf16[64,768]{1,0:T(8,128)(2,1)S(1)}, u32[]{:S(2)}, u32[]{:S(2)}) collective-permute-start(bf16[64,768]{1,0:T(8,128)(2,1)S(1)} %get-tuple-element.115), channel_id=1, source_target_pairs={{0,8},{1,9},{2,10},{3,11},{4,12},{5,13},{6,14},{7,15},{8,16},{9,17... | collective-permute-start | bytes 294920 | tf_op jit(solution)/shard_map/ppermute | solution.py:258
  433.5 10.0 %collective-permute-start.17 = (bf16[64,768]{1,0:T(8,128)(2,1)S(1)}, bf16[64,768]{1,0:T(8,128)(2,1)S(1)}, u32[]{:S(2)}, u32[]{:S(2)}) collective-permute-start(bf16[64,768]{1,0:T(8,128)(2,1)S(1)} %get-tuple-element.116), channel_id=1, source_target_pairs={{0,24},{1,25},{2,26},{3,27},{4,28},{5,29},{6,30},{7,31},{8,0},{9,1... | collective-permute-start | bytes 294920 | tf_op jit(solution)/shard_map/ppermute | solution.py:258
  442.2 24.1 %collective-permute-start.26 = (bf16[4,96,768]{2,1,0:T(8,128)(2,1)S(1)}, bf16[4,96,768]{2,1,0:T(8,128)(2,1)S(1)}, u32[]{:S(2)}, u32[]{:S(2)}) collective-permute-start(bf16[4,96,768]{2,1,0:T(8,128)(2,1)S(1)} %dynamic-slice_bitcast_fusion.4), channel_id=1, source_target_pairs={{0,2},{1,3},{2,0},{3,1},{4,6},{5,7},{6,4},{7,5},{8,10},{9,11},{10,... | collective-permute-start | bytes 1769480 | tf_op jit(solution)/shard_map/ppermute | solution.py:258
  466.5 7.1 %collective-permute-start.27 = (bf16[96,768]{1,0:T(8,128)(2,1)S(1)}, bf16[96,768]{1,0:T(8,128)(2,1)S(1)}, u32[]{:S(2)}, u32[]{:S(2)}) collective-permute-start(bf16[96,768]{1,0:T(8,128)(2,1)S(1)} %get-tuple-element.112), channel_id=1, source_target_pairs={{0,8},{1,9},{2,10},{3,11},{4,12},{5,13},{6,14},{7,15},{8,16},{9,17... | collective-permute-start | bytes 442376 | tf_op jit(solution)/shard_map/ppermute | solution.py:258
  466.6 7.0 %collective-permute-start.29 = (bf16[96,768]{1,0:T(8,128)(2,1)S(1)}, bf16[96,768]{1,0:T(8,128)(2,1)S(1)}, u32[]{:S(2)}, u32[]{:S(2)}) collective-permute-start(bf16[96,768]{1,0:T(8,128)(2,1)S(1)} %get-tuple-element.113), channel_id=1, source_target_pairs={{0,24},{1,25},{2,26},{3,27},{4,28},{5,29},{6,30},{7,31},{8,0},{9,1... | collective-permute-start | bytes 442376 | tf_op jit(solution)/shard_map/ppermute | solution.py:258
  470.4 12.5 %collective-permute-start.28 = (bf16[96,768]{1,0:T(8,128)(2,1)S(1)}, bf16[96,768]{1,0:T(8,128)(2,1)S(1)}, u32[]{:S(2)}, u32[]{:S(2)}) collective-permute-start(bf16[96,768]{1,0:T(8,128)(2,1)S(1)} %get-tuple-element.114), channel_id=1, source_target_pairs={{0,16},{1,17},{2,18},{3,19},{4,20},{5,21},{6,22},{7,23},{8,24},{9,... | collective-permute-start | bytes 442376 | tf_op jit(solution)/shard_map/ppermute | solution.py:258
  470.8 12.1 %collective-permute-start.32 = (bf16[4,112,768]{2,1,0:T(8,128)(2,1)S(1)}, bf16[4,112,768]{2,1,0:T(8,128)(2,1)S(1)}, u32[]{:S(2)}, u32[]{:S(2)}) collective-permute-start(bf16[4,112,768]{2,1,0:T(8,128)(2,1)S(1)} %dynamic-slice_bitcast_fusion.3), channel_id=1, source_target_pairs={{0,4},{1,5},{2,6},{3,7},{4,0},{5,1},{6,2},{7,3},{8,12},{9,13},{10,... | collective-permute-start | bytes 2064392 | tf_op jit(solution)/shard_map/ppermute | solution.py:258
  483.2 7.4 %collective-permute-start.33 = (bf16[112,768]{1,0:T(8,128)(2,1)S(1)}, bf16[112,768]{1,0:T(8,128)(2,1)S(1)}, u32[]{:S(2)}, u32[]{:S(2)}) collective-permute-start(bf16[112,768]{1,0:T(8,128)(2,1)S(1)} %get-tuple-element.109), channel_id=1, source_target_pairs={{0,8},{1,9},{2,10},{3,11},{4,12},{5,13},{6,14},{7,15},{8,16},{9,17... | collective-permute-start | bytes 516104 | tf_op jit(solution)/shard_map/ppermute | solution.py:258
  483.3 7.5 %collective-permute-start.35 = (bf16[112,768]{1,0:T(8,128)(2,1)S(1)}, bf16[112,768]{1,0:T(8,128)(2,1)S(1)}, u32[]{:S(2)}, u32[]{:S(2)}) collective-permute-start(bf16[112,768]{1,0:T(8,128)(2,1)S(1)} %get-tuple-element.110), channel_id=1, source_target_pairs={{0,24},{1,25},{2,26},{3,27},{4,28},{5,29},{6,30},{7,31},{8,0},{9,1... | collective-permute-start | bytes 516104 | tf_op jit(solution)/shard_map/ppermute | solution.py:258
  487.1 8.9 %collective-permute-start.34 = (bf16[112,768]{1,0:T(8,128)(2,1)S(1)}, bf16[112,768]{1,0:T(8,128)(2,1)S(1)}, u32[]{:S(2)}, u32[]{:S(2)}) collective-permute-start(bf16[112,768]{1,0:T(8,128)(2,1)S(1)} %get-tuple-element.111), channel_id=1, source_target_pairs={{0,16},{1,17},{2,18},{3,19},{4,20},{5,21},{6,22},{7,23},{8,24},{9,... | collective-permute-start | bytes 516104 | tf_op jit(solution)/shard_map/ppermute | solution.py:258
  (52 other events, 266.2 us)
Sparse Core Ops, SparseCore 0:
  13.0 99.3 all-gather.1

commit v3 on v2

--- a/solution.py
+++ b/solution.py
@@ -116,7 +116,7 @@
     return (output.astype(jnp.bfloat16), stored)
 
 
-def backward_pass(stored, cotangent_micro, attention_full, feed_full):
+def backward_pass(stored, cotangent_micro, attention_full, feed_full, feed_reduce):
     (
         query_weight,
         key_weight,
@@ -183,6 +183,15 @@
     grad_values = merge_heads(grad_values).astype(jnp.bfloat16)
     row_delta = jnp.sum(grad_probs * probs, axis=-1, keepdims=True)
     grad_scores = (probs * (grad_probs - row_delta)).astype(jnp.bfloat16)
+    feed_terms = (
+        up_weight_term,
+        down_weight_term,
+        up_bias_term,
+        down_bias_term,
+        second_gain_term,
+        second_shift_term,
+    )
+    grad_scores, feed_sums = lax.optimization_barrier((grad_scores, feed_reduce(feed_terms)))
     score_scale = 1.0 / math.sqrt(HEAD_DIM)
     grad_queries = jnp.einsum(
         "shqk,skhd->sqhd", grad_scores, key_heads, preferred_element_type=jnp.float32
@@ -212,15 +221,7 @@
         first_gain_term,
         first_shift_term,
     )
-    feed_terms = (
-        up_weight_term,
-        down_weight_term,
-        up_bias_term,
-        down_bias_term,
-        second_gain_term,
-        second_shift_term,
-    )
-    return (input_grad, attention_terms, feed_terms)
+    return (input_grad, attention_terms, feed_sums)
 
 
 def axis_sizes(device_count):
@@ -383,30 +384,32 @@
     attention_full = tuple(square) + tuple(part.reshape(-1) for part in lines)
 
     output, stored = forward_pass(tokens, lengths, attention_full, feed_full)
-    input_grad, attention_terms, feed_terms = backward_pass(
-        stored, cotangent, attention_full, feed_full
-    )
-
     def to_blocks(matrix):
         return matrix.reshape(device_count, -1, width)
 
     def to_lines(vector):
         return vector.reshape(device_count, -1)
 
-    up_term, down_term, up_bias_term, down_bias_term, gain_term, shift_term = feed_terms
-    down_packed = pack_rows(
-        [to_blocks(down_term)],
-        [to_lines(part) for part in (up_bias_term, down_bias_term, gain_term, shift_term)],
-        width,
-        jnp.bfloat16,
-    )
-    down_sum = scatter_sum(down_packed, sizes, X_FIRST)
-    up_sum = scatter_sum(
-        jnp.concatenate(
-            [part.astype(jnp.bfloat16) for part in up_pieces(up_term, device_count)], axis=1
-        ),
-        sizes,
-        Y_FIRST,
+    def feed_reduce(feed_terms):
+        up_term, down_term, up_bias_term, down_bias_term, gain_term, shift_term = feed_terms
+        down_packed = pack_rows(
+            [to_blocks(down_term)],
+            [to_lines(part) for part in (up_bias_term, down_bias_term, gain_term, shift_term)],
+            width,
+            jnp.bfloat16,
+        )
+        down_sum = scatter_sum(down_packed, sizes, X_FIRST)
+        up_sum = scatter_sum(
+            jnp.concatenate(
+                [part.astype(jnp.bfloat16) for part in up_pieces(up_term, device_count)], axis=1
+            ),
+            sizes,
+            Y_FIRST,
+        )
+        return (down_sum, up_sum)
+
+    input_grad, attention_terms, (down_sum, up_sum) = backward_pass(
+        stored, cotangent, attention_full, feed_full, feed_reduce
     )
     query_term, key_term, value_term, out_term = [to_blocks(part) for part in attention_terms[:4]]
     far_sum = scatter_sum(

time: 509 us -> 517 us (1.016)
  waiting for transfers between devices: 116 us -> 132 us
  other arithmetic: 58.6 us -> 49.1 us
  starting transfers between devices: 49.6 us -> 41.5 us
  matrix products: 169 us -> 175 us
    sub x0 -> x1, matrix products: none -> 31 us  [backward_pass(): grad_scores = (probs * (grad_probs - row_delta)).astype(jnp.bfloat16)]
    convert_element_type x1 -> x0, other arithmetic: 21.8 us -> none  [backward_pass(): grad_scores = (probs * (grad_probs - row_delta)).astype(jnp.bfloat16)]
    dot_general x1 -> x0, matrix products: 19.7 us -> none  [backward_pass(): jnp.einsum('sqhd,skhd->shqk', grad_context, value_heads, preferred_elemen...]
    ppermute x12, starting transfers between devices: 21.7 us -> 11.4 us  [gather_blocks(): part = lax.ppermute(held, 'fsdp', shifted_pairs(sizes, axis, shift))]
    ppermute x24, waiting for transfers between devices: 81.2 us -> 90.1 us  [scatter_sum(): lax.ppermute(part, 'fsdp', shifted_pairs(sizes, axis, shift))]
    convert_element_type x12, other arithmetic: 11.2 us -> 19 us  [scatter_sum(): held = held.astype(jnp.bfloat16)]
    ppermute x12, waiting for transfers between devices: 34.3 us -> 41.8 us  [gather_blocks(): part = lax.ppermute(held, 'fsdp', shifted_pairs(sizes, axis, shift))]
    squeeze x12, local copies, waits for them, and re-layouts: 1.42 us -> 6.86 us  [scatter_sum(): part = lax.dynamic_index_in_dim(held, target, place, keepdims=False)]
  transfers between devices with their start and end apart: 37 -> 37, of which waited for: 18 -> 15; matrix products, arithmetic and copies ran while one was open for 25% -> 35% of each run, Pallas kernels for 0% -> 0%
where the time goes in v3:
time: 517 us; the launch traced here: 513 us
  matrix products  175 us (34%)
  waiting for transfers between devices  132 us (26%)
  local copies, waits for them, and re-layouts  99.1 us (19%)
  other arithmetic  49.1 us (9%)
  starting transfers between devices  41.5 us (8%)
  between operations  15.8 us (3%)
    ppermute x24, waiting for transfers between devices, scatter_sum(): lax.ppermute(part, 'fsdp', shifted_pairs(sizes, axis, shift))  90.1 us
    ppermute x12, waiting for transfers between devices, gather_blocks(): part = lax.ppermute(held, 'fsdp', shifted_pairs(sizes, axis, shift))  41.8 us
    dot_general x6, matrix products, times_back(): lax.dot_general(left_side, right_side, (((1,), (1,)), ((), ())), preferre...  33.1 us
    dot_general x6, matrix products, times_plain(): return jnp.dot(left_side, right_side, preferred_element_type=jnp.float32)  32.9 us
    unnamed x148, local copies, waits for them, and re-layouts  32.4 us
    sub x1, matrix products, backward_pass(): grad_scores = (probs * (grad_probs - row_delta)).astype(jnp.bfloat16)  31 us
    ppermute x24, starting transfers between devices, scatter_sum(): lax.ppermute(part, 'fsdp', shifted_pairs(sizes, axis, shift))  30.1 us
    dot_general x6, matrix products, times_across(): lax.dot_general(left_side, right_side, (((0,), (0,)), ((), ())), preferre...  28.2 us
  transfers between devices with their start and end apart: 37, of which 15 were waited for; matrix products, arithmetic and copies ran while one was open for 35% of the time, Pallas kernels for 0%

profile of v3, /device:TPU:0, one launch (start us, length us, event | category | flops | bytes accessed | tf_op | source)
XLA Modules:
  0.0 512.7 jit_solution(12238088966415981240)
XLA Ops:
  24.4 5.7 %collective-permute-done = bf16[48,768]{1,0:T(8,128)(2,1)S(1)} collective-permute-done((bf16[48,768]{1,0:T(8,128)(2,1)S(1)}, bf16[48,768]{1,0:T(8,128)(2,1)S(1)}, u32[]{:S(2)}, u32[]{:S(2)}) %collective-permute-start) | collective-permute-done | bytes 73760 | tf_op jit(solution)/shard_map/ppermute | solution.py:279
  30.2 9.7 %collective-permute-done.1 = bf16[48,768]{1,0:T(8,128)(2,1)S(1)} collective-permute-done((bf16[48,768]{1,0:T(8,128)(2,1)S(1)}, bf16[48,768]{1,0:T(8,128)(2,1)S(1)}, u32[]{:S(2)}, u32[]{:S(2)}) %collective-permute-start.1) | collective-permute-done | bytes 73760 | tf_op jit(solution)/shard_map/ppermute | solution.py:279
  45.6 6.1 %collective-permute-done.3 = bf16[4,48,768]{2,1,0:T(8,128)(2,1)S(1)} collective-permute-done((bf16[4,48,768]{2,1,0:T(8,128)(2,1)S(1)}, bf16[4,48,768]{2,1,0:T(8,128)(2,1)S(1)}, u32[]{:S(2)}, u32[]{:S(2)}) %collective-permute-start.3) | collective-permute-done | bytes 294944 | tf_op jit(solution)/shard_map/ppermute | solution.py:279
  51.9 8.8 %collective-permute-done.9 = bf16[4,64,768]{2,1,0:T(8,128)(2,1)S(1)} collective-permute-done((bf16[4,64,768]{2,1,0:T(8,128)(2,1)S(1)}, bf16[4,64,768]{2,1,0:T(8,128)(2,1)S(1)}, u32[]{:S(2)}, u32[]{:S(2)}) %collective-permute-start.9) | collective-permute-done | bytes 393248 | tf_op jit(solution)/shard_map/ppermute | solution.py:279
  65.1 4.2 collective-permute-done.4
  70.2 4.9 collective-permute-done.10
  96.3 4.4 fusion.49
  103.7 5.0 fusion.48
  108.7 4.0 reshape.414
  112.7 11.2 %fusion.3 = (f32[2,12,512]{2,1,0:T(8,128)S(1)}, f32[2,12,512,512]{2,3,1,0:T(8,128)}) fusion(pred[2,512]{1,0:T(4,128)(4,1)S(1)} %get-tuple-element.148, bf16[2,512,12,64]{1,0,3,2:T(2,128)(2,1)S(1)} %reshape.418, bf16[2,512,12,64]{1,0,3,2:T(2,128)(2,1)S(1)} %reshape.416), kind=kOutput, calls=%fused_computation.9 | convolution fusion | flops 824168448 | bytes 28361728 | tf_op jit(solution)/shard_map/sqhd,skhd->shqk/dot_general | solution.py:53
  123.9 11.2 %fusion.2 = f32[2,12,512]{2,1,0:T(8,128)S(1)} fusion(f32[2,12,512,512]{2,3,1,0:T(8,128)} %get-tuple-element.150, f32[2,12,512]{2,1,0:T(8,128)S(1)} %get-tuple-element.149, pred[2,512]{1,0:T(4,128)(4,1)S(1)} %get-tuple-element.148), kind=kLoop, calls=%fused_computation.8 | loop fusion | flops 25153536 | bytes 25265152 | tf_op jit(solution)/shard_map/reduce_sum | solution.py:87
  135.1 11.9 %fusion.50 = bf16[2,512,12,64]{1,3,2,0:T(8,128)(2,1)S(1)} fusion(f32[2,12,512,512]{2,3,1,0:T(8,128)} %get-tuple-element.150, f32[2,12,512]{2,1,0:T(8,128)S(1)} %fusion.2, f32[2,12,512]{2,1,0:T(8,128)S(1)} %get-tuple-element.149, pred[2,512]{1,0:T(4,128)(4,1)S(1)} %get-tuple-element.148, bf16[2,512,12,64]{1,0,3,2:T(2,128)(2,1)S(1)} %copy-done.34), kind=kOutput, calls=%fused_computation.104 | convolution fusion | flops 837550080 | bytes 28410880 | tf_op jit(solution)/shard_map/shqk,skhd->sqhd/dot_general | solution.py:90
  150.4 3.8 fusion.116
  161.1 11.3 %multiply_convert_fusion.1 = (bf16[1024,3072]{1,0:T(8,128)(2,1)S(1)}, f32[1024,3072]{1,0:T(8,128)}) fusion(f32[3072]{0:T(1024)S(1)} %reshape.439, bf16[768,768]{1,0:T(8,128)(2,1)S(1)} %bitcast.366, bf16[768,768]{1,0:T(8,128)(2,1)S(1)} %bitcast.368, bf16[768,768]{1,0:T(8,128)(2,1)S(1)} %bitcast.370, bf16[768,768]{1,0:T(8,128)(2,1)S(1)} %bitcast.364, ...), kind=kOutput, calls=%fused_computation.13 | convolution fusion | flops 4873519104 | bytes 26765312 | tf_op jit(solution)/shard_map/dot_general | solution.py:24
  172.4 5.0 slice.212
  178.0 5.9 %fusion.117 = (f32[1024]{0:T(1024)S(1)}, f32[1024,768]{0,1:T(8,128)S(1)}) fusion(f32[768]{0:T(1024)S(1)} %reshape.440, bf16[1024,3072]{1,0:T(8,128)(2,1)S(1)} %get-tuple-element.153, bf16[3072,768]{1,0:T(8,128)(2,1)S(1)} %bitcast.346, f32[768]{0:T(1024)S(1)} %reshape.438, f32[768]{0:T(1024)S(1)} %reshape.437, f32[1024]{0:T(1024)S(1)} %fusion.93, ...), kind=kOutput, calls=%fused_computation.259 | convolution fusion | flops 4837342208 | bytes 17323008 | tf_op jit(solution)/shard_map/dot_general | solution.py:24
  190.8 10.6 %convolution_convert_fusion.1 = bf16[3072,768]{1,0:T(8,128)(2,1)} fusion(bf16[1024,3072]{1,0:T(8,128)(2,1)} %copy-done.53, bf16[1024,768]{0,1:T(8,128)(2,1)S(1)} %get-tuple-element.85), kind=kOutput, calls=%fused_computation.28 | convolution fusion | flops 4834197504 | bytes 12582912 | tf_op jit(solution)/shard_map/dot_general | solution.py:28
  201.5 13.6 %fusion.118 = (bf16[3072]{0:T(1024)(128)(2,1)S(1)}, bf16[1024,3072]{1,0:T(8,128)(2,1)}) fusion(f32[1024,3072]{1,0:T(8,128)S(1)} %bitcast.402, f32[3072]{0:T(1024)S(1)} %reshape.439, bf16[1024,768]{0,1:T(8,128)(2,1)S(1)} %get-tuple-element.85, bf16[3072,768]{1,0:T(8,128)(2,1)S(1)} %bitcast.349), kind=kOutput, calls=%fused_computation.260 | convolution fusion | flops 4875875328 | bytes 25184256 | tf_op jit(solution)/shard_map/dot_general | solution.py:34
  215.1 9.6 %multiply_reduce_fusion.1 = (bf16[768]{0:T(1024)(128)(2,1)S(1)}, f32[1024]{0:T(1024)S(1)}, bf16[768]{0:T(1024)(128)(2,1)S(1)}, f32[1024,768]{0,1:T(8,128)S(1)}) fusion(f32[1024,768]{0,1:T(8,128)S(1)} %copy-done.7, f32[1024]{0:T(1024)S(1)} %fusion.93, f32[1024]{0:T(1024)S(1)} %broadcast_multiply_fusion.1, f32[768]{0:T(1024)S(1)} %reshape.437, ...), kind=kOutput, calls=%fused_computation.38 | convolution fusion | flops 4864865280 | bytes 22062080 | tf_op jit(solution)/shard_map/dot_general | solution.py:34
  224.7 9.8 %convolution_convert_fusion = bf16[768,3072]{1,0:T(8,128)(2,1)} fusion(bf16[1024,3072]{1,0:T(8,128)(2,1)} %get-tuple-element.159, f32[1024,768]{0,1:T(8,128)S(1)} %copy-done.7, f32[768]{0:T(1024)S(1)} %reshape.438, f32[768]{0:T(1024)S(1)} %reshape.437, f32[1024]{0:T(1024)S(1)} %fusion.93, f32[1024]{0:T(1024)S(1)} %broadcast_multiply_fusion.1), kind=kOutput, calls=%fused_computation.27 | convolution fusion | flops 4838129664 | bytes 14170112 | tf_op jit(solution)/shard_map/dot_general | solution.py:28
  242.0 4.0 reshape.431
  246.7 3.8 fusion.21
  257.4 11.4 %fusion.120 = (bf16[12,64]{1,0:T(8,128)(2,1)S(1)}, bf16[2,512,12,64]{1,3,2,0:T(8,128)(2,1)S(1)}) fusion(f32[2,12,512,512]{2,3,1,0:T(8,128)} %get-tuple-element.150, f32[2,12,512]{2,1,0:T(8,128)S(1)} %log_add_fusion, pred[2,512]{1,0:T(4,128)(4,1)S(1)} %get-tuple-element.148, bf16[2,512,12,64]{1,0,3,2:T(2,128)(2,1)S(1)} %copy-done.35), kind=kOutput, calls=%fused_computation.262 | convolution fusion | flops 832044288 | bytes 28363264 | tf_op jit(solution)/shard_map/shqk,sqhd->skhd/dot_general | solution.py:177
  295.1 42.0 %collective-permute-done.31 = bf16[4,2,48,768]{3,2,1,0:T(8,128)(2,1)} collective-permute-done((bf16[4,2,48,768]{3,2,1,0:T(8,128)(2,1)}, bf16[4,2,48,768]{3,2,1,0:T(8,128)(2,1)}, u32[]{:S(2)}, u32[]{:S(2)}) %collective-permute-start.31) | collective-permute-done | bytes 589856 | tf_op jit(solution)/shard_map/ppermute | solution.py:259
  349.0 31.0 %multiply_convert_fusion = bf16[2,12,512,512]{2,3,1,0:T(8,128)(2,1)} fusion(f32[2,12,512,512]{2,3,1,0:T(8,128)} %get-tuple-element.150, f32[2,12,512]{2,1,0:T(8,128)S(1)} %log_add_fusion, pred[2,512]{1,0:T(4,128)(4,1)S(1)} %get-tuple-element.148, bf16[2,512,12,64]{1,0,3,2:T(2,128)(2,1)} %reshape.431, bf16[2,512,12,64]{1,0,3,2:T(2,128)(2,1)} %reshape.414), kind=kOutput, calls=%fused_computation.1 | convolution fusion | flops 1673540096 | bytes 40944640 | tf_op jit(solution)/shard_map/sub | solution.py:185
  393.5 5.2 %collective-permute-start.15 = (bf16[112,768]{1,0:T(8,128)(2,1)S(1)}, bf16[112,768]{1,0:T(8,128)(2,1)S(1)}, u32[]{:S(2)}, u32[]{:S(2)}) collective-permute-start(bf16[112,768]{1,0:T(8,128)(2,1)S(1)} %get-tuple-element.115), channel_id=1, source_target_pairs={{0,8},{1,9},{2,10},{3,11},{4,12},{5,13},{6,14},{7,15},{8,16},{9,17... | collective-permute-start | bytes 516104 | tf_op jit(solution)/shard_map/ppermute | solution.py:259
  398.7 11.0 %collective-permute-done.22 = bf16[96,768]{1,0:T(8,128)(2,1)S(1)} collective-permute-done((bf16[96,768]{1,0:T(8,128)(2,1)S(1)}, bf16[96,768]{1,0:T(8,128)(2,1)S(1)}, u32[]{:S(2)}, u32[]{:S(2)}) %collective-permute-start.22) | collective-permute-done | bytes 147488 | tf_op jit(solution)/shard_map/ppermute | solution.py:259
  410.5 4.0 collective-permute-done.16
  414.6 8.6 %fusion.46 = bf16[2,512,12,64]{1,3,2,0:T(8,128)(2,1)S(1)} fusion(bf16[2,12,512,512]{2,3,1,0:T(8,128)(2,1)} %multiply_convert_fusion, bf16[2,512,12,64]{1,0,3,2:T(2,128)(2,1)S(1)} %copy-done.4), kind=kOutput, calls=%fused_computation.100 | convolution fusion | flops 806879232 | bytes 15728640 | tf_op jit(solution)/shard_map/shqk,sqhd->skhd/dot_general | solution.py:200
  423.2 6.8 %fusion.119 = (bf16[12,64]{1,0:T(8,128)(2,1)S(1)}, bf16[2,512,12,64]{1,3,2,0:T(8,128)(2,1)S(1)}) fusion(bf16[2,12,512,512]{2,3,1,0:T(8,128)(2,1)} %multiply_convert_fusion, bf16[2,512,12,64]{1,0,3,2:T(2,128)(2,1)S(1)} %copy-done.2), kind=kOutput, calls=%fused_computation.261 | convolution fusion | flops 807664896 | bytes 15730176 | tf_op jit(solution)/shard_map/shqk,skhd->sqhd/dot_general | solution.py:196
  468.9 15.6 %collective-permute-done.25 = bf16[4,2,64,768]{3,2,0,1:T(8,128)(2,1)S(1)} collective-permute-done((bf16[4,2,64,768]{3,2,0,1:T(8,128)(2,1)S(1)}, bf16[4,2,64,768]{3,2,0,1:T(8,128)(2,1)S(1)}, u32[]{:S(2)}, u32[]{:S(2)}) %collective-permute-start.25) | collective-permute-done | bytes 786464 | tf_op jit(solution)/shard_map/ppermute | solution.py:259
  486.7 8.2 %collective-permute-done.26 = bf16[4,64,768]{2,1,0:T(8,128)(2,1)S(1)} collective-permute-done((bf16[4,64,768]{2,1,0:T(8,128)(2,1)S(1)}, bf16[4,64,768]{2,1,0:T(8,128)(2,1)S(1)}, u32[]{:S(2)}, u32[]{:S(2)}) %collective-permute-start.26) | collective-permute-done | bytes 393248 | tf_op jit(solution)/shard_map/ppermute | solution.py:259
  (351 shorter events, 188.6 us)
Async XLA Ops:
  7.2 147.5 %all-gather.2.cloned.1.call-start = ((), (), s32[]{:S(2)}) async-start(), calls=%async_computation | async-start | bytes 10543104 | tf_op jit(solution)/shard_map/all_gather | solution.py:352
  14.6 29.3 %collective-permute-start.6 = (bf16[64,768]{1,0:T(8,128)(2,1)S(1)}, bf16[64,768]{1,0:T(8,128)(2,1)S(1)}, u32[]{:S(2)}, u32[]{:S(2)}) collective-permute-start(bf16[64,768]{1,0:T(8,128)(2,1)S(1)} %get-tuple-element.135), channel_id=1, source_target_pairs={{0,8},{1,9},{2,10},{3,11},{4,12},{5,13},{6,14},{7,15},{8,16},{9,17... | collective-permute-start | bytes 294920 | tf_op jit(solution)/shard_map/ppermute | solution.py:279
  17.7 26.3 %collective-permute-start.7 = (bf16[64,768]{1,0:T(8,128)(2,1)S(1)}, bf16[64,768]{1,0:T(8,128)(2,1)S(1)}, u32[]{:S(2)}, u32[]{:S(2)}) collective-permute-start(bf16[64,768]{1,0:T(8,128)(2,1)S(1)} %get-tuple-element.135), channel_id=1, source_target_pairs={{0,16},{1,17},{2,18},{3,19},{4,20},{5,21},{6,22},{7,23},{8,24},{9,... | collective-permute-start | bytes 294920 | tf_op jit(solution)/shard_map/ppermute | solution.py:279
  20.3 23.7 %collective-permute-start.8 = (bf16[64,768]{1,0:T(8,128)(2,1)S(1)}, bf16[64,768]{1,0:T(8,128)(2,1)S(1)}, u32[]{:S(2)}, u32[]{:S(2)}) collective-permute-start(bf16[64,768]{1,0:T(8,128)(2,1)S(1)} %get-tuple-element.135), channel_id=1, source_target_pairs={{0,24},{1,25},{2,26},{3,27},{4,28},{5,29},{6,30},{7,31},{8,0},{9,1... | collective-permute-start | bytes 294920 | tf_op jit(solution)/shard_map/ppermute | solution.py:279
  23.9 16.0 %collective-permute-start.1 = (bf16[48,768]{1,0:T(8,128)(2,1)S(1)}, bf16[48,768]{1,0:T(8,128)(2,1)S(1)}, u32[]{:S(2)}, u32[]{:S(2)}) collective-permute-start(bf16[48,768]{1,0:T(8,128)(2,1)S(1)} %constant_dynamic-update-slice_fusion), channel_id=1, source_target_pairs={{0,16},{1,17},{2,18},{3,19},{4,20},{5,21},{6,22},{7,23},{8,24},{9,... | collective-permute-start | bytes 221192 | tf_op jit(solution)/shard_map/ppermute | solution.py:279
  30.2 12.1 %collective-permute-start.2 = (bf16[48,768]{1,0:T(8,128)(2,1)S(1)}, bf16[48,768]{1,0:T(8,128)(2,1)S(1)}, u32[]{:S(2)}, u32[]{:S(2)}) collective-permute-start(bf16[48,768]{1,0:T(8,128)(2,1)S(1)} %constant_dynamic-update-slice_fusion), channel_id=1, source_target_pairs={{0,24},{1,25},{2,26},{3,27},{4,28},{5,29},{6,30},{7,31},{8,0},{9,1... | collective-permute-start | bytes 221192 | tf_op jit(solution)/shard_map/ppermute | solution.py:279
  42.3 9.3 %collective-permute-start.3 = (bf16[4,48,768]{2,1,0:T(8,128)(2,1)S(1)}, bf16[4,48,768]{2,1,0:T(8,128)(2,1)S(1)}, u32[]{:S(2)}, u32[]{:S(2)}) collective-permute-start(bf16[4,48,768]{2,1,0:T(8,128)(2,1)S(1)} %bitcast_dynamic-update-slice_fusion.16), channel_id=1, source_target_pairs={{0,2},{1,3},{2,0},{3,1},{4,6},{5,7},{6,4},{7,5},{8,10},{9,11},{10,... | collective-permute-start | bytes 884744 | tf_op jit(solution)/shard_map/ppermute | solution.py:279
  44.1 16.7 %collective-permute-start.9 = (bf16[4,64,768]{2,1,0:T(8,128)(2,1)S(1)}, bf16[4,64,768]{2,1,0:T(8,128)(2,1)S(1)}, u32[]{:S(2)}, u32[]{:S(2)}) collective-permute-start(bf16[4,64,768]{2,1,0:T(8,128)(2,1)S(1)} %bitcast_dynamic-update-slice_fusion.13), channel_id=1, source_target_pairs={{0,4},{1,5},{2,6},{3,7},{4,0},{5,1},{6,2},{7,3},{8,12},{9,13},{10,... | collective-permute-start | bytes 1179656 | tf_op jit(solution)/shard_map/ppermute | solution.py:279
  51.6 17.7 %collective-permute-start.4 = (bf16[4,2,48,768]{3,2,1,0:T(8,128)(2,1)S(1)}, bf16[4,2,48,768]{3,2,1,0:T(8,128)(2,1)S(1)}, u32[]{:S(2)}, u32[]{:S(2)}) collective-permute-start(bf16[4,2,48,768]{3,2,1,0:T(8,128)(2,1)S(1)} %bitcast_dynamic-update-slice_fusion.11), channel_id=1, source_target_pairs={{0,4},{1,5},{2,6},{3,7},{4,0},{5,1},{6,2},{7,3},{8,12},{9,13},{10,... | collective-permute-start | bytes 1769480 | tf_op jit(solution)/shard_map/ppermute | solution.py:279
  60.8 14.3 %collective-permute-start.10 = (bf16[4,2,64,768]{3,2,1,0:T(8,128)(2,1)S(1)}, bf16[4,2,64,768]{3,2,1,0:T(8,128)(2,1)S(1)}, u32[]{:S(2)}, u32[]{:S(2)}) collective-permute-start(bf16[4,2,64,768]{3,2,1,0:T(8,128)(2,1)S(1)} %bitcast_dynamic-update-slice_fusion.9), channel_id=1, source_target_pairs={{0,2},{1,3},{2,0},{3,1},{4,6},{5,7},{6,4},{7,5},{8,10},{9,11},{10,... | collective-permute-start | bytes 2359304 | tf_op jit(solution)/shard_map/ppermute | solution.py:279
  70.2 13.1 %collective-permute-start.5 = (bf16[4,2,2,48,768]{4,3,2,1,0:T(8,128)(2,1)}, bf16[4,2,2,48,768]{4,3,2,1,0:T(8,128)(2,1)}, u32[]{:S(2)}, u32[]{:S(2)}) collective-permute-start(bf16[4,2,2,48,768]{4,3,2,1,0:T(8,128)(2,1)} %bitcast_dynamic-update-slice_fusion.7), channel_id=1, source_target_pairs={{0,1},{1,0},{2,3},{3,2},{4,5},{5,4},{6,7},{7,6},{8,9},{9,8},{10,11... | collective-permute-start | bytes 3538952 | tf_op jit(solution)/shard_map/ppermute | solution.py:279
  76.0 10.3 %collective-permute-start.11 = (bf16[4,2,2,64,768]{4,3,2,1,0:T(8,128)(2,1)}, bf16[4,2,2,64,768]{4,3,2,1,0:T(8,128)(2,1)}, u32[]{:S(2)}, u32[]{:S(2)}) collective-permute-start(bf16[4,2,2,64,768]{4,3,2,1,0:T(8,128)(2,1)} %bitcast_dynamic-update-slice_fusion.5), channel_id=1, source_target_pairs={{0,1},{1,0},{2,3},{3,2},{4,5},{5,4},{6,7},{7,6},{8,9},{9,8},{10,11... | collective-permute-start | bytes 4718600 | tf_op jit(solution)/shard_map/ppermute | solution.py:279
  252.2 34.8 %collective-permute-start.12 = (bf16[4,2,2,112,768]{4,3,0,1,2:T(8,128)(2,1)}, bf16[4,2,2,112,768]{4,3,0,1,2:T(8,128)(2,1)}, u32[]{:S(2)}, u32[]{:S(2)}) collective-permute-start(bf16[4,2,2,112,768]{4,3,0,1,2:T(8,128)(2,1)} %bitcast.325), channel_id=1, source_target_pairs={{0,1},{1,0},{2,3},{3,2},{4,5},{5,4},{6,7},{7,6},{8,9},{9,8},{10,11... | collective-permute-start | bytes 8257544 | tf_op jit(solution)/shard_map/ppermute | solution.py:259
  256.8 24.4 %collective-permute-start.18 = (bf16[4,2,2,96,768]{4,3,0,2,1:T(8,128)(2,1)}, bf16[4,2,2,96,768]{4,3,0,2,1:T(8,128)(2,1)}, u32[]{:S(2)}, u32[]{:S(2)}) collective-permute-start(bf16[4,2,2,96,768]{4,3,0,2,1:T(8,128)(2,1)} %bitcast.326), channel_id=1, source_target_pairs={{0,1},{1,0},{2,3},{3,2},{4,5},{5,4},{6,7},{7,6},{8,9},{9,8},{10,11... | collective-permute-start | bytes 7077896 | tf_op jit(solution)/shard_map/ppermute | solution.py:259
  285.4 54.6 %collective-permute-start.19 = (bf16[4,2,96,768]{3,2,0,1:T(8,128)(2,1)}, bf16[4,2,96,768]{3,2,0,1:T(8,128)(2,1)}, u32[]{:S(2)}, u32[]{:S(2)}) collective-permute-start(bf16[4,2,96,768]{3,2,0,1:T(8,128)(2,1)} %dynamic-slice_bitcast_fusion.1), channel_id=1, source_target_pairs={{0,4},{1,5},{2,6},{3,7},{4,0},{5,1},{6,2},{7,3},{8,12},{9,13},{10,... | collective-permute-start | bytes 3538952 | tf_op jit(solution)/shard_map/ppermute | solution.py:259
  292.2 52.0 %collective-permute-start.13 = (bf16[4,2,112,768]{3,2,0,1:T(8,128)(2,1)}, bf16[4,2,112,768]{3,2,0,1:T(8,128)(2,1)}, u32[]{:S(2)}, u32[]{:S(2)}) collective-permute-start(bf16[4,2,112,768]{3,2,0,1:T(8,128)(2,1)} %dynamic-slice_bitcast_fusion), channel_id=1, source_target_pairs={{0,2},{1,3},{2,0},{3,1},{4,6},{5,7},{6,4},{7,5},{8,10},{9,11},{10,... | collective-permute-start | bytes 4128776 | tf_op jit(solution)/shard_map/ppermute | solution.py:259
  294.2 42.9 %collective-permute-start.31 = (bf16[4,2,48,768]{3,2,1,0:T(8,128)(2,1)}, bf16[4,2,48,768]{3,2,1,0:T(8,128)(2,1)}, u32[]{:S(2)}, u32[]{:S(2)}) collective-permute-start(bf16[4,2,48,768]{3,2,1,0:T(8,128)(2,1)} %dynamic-slice_bitcast_fusion.4), channel_id=1, source_target_pairs={{0,2},{1,3},{2,0},{3,1},{4,6},{5,7},{6,4},{7,5},{8,10},{9,11},{10,... | collective-permute-start | bytes 1769480 | tf_op jit(solution)/shard_map/ppermute | solution.py:259
  339.3 41.2 %collective-permute-start.32 = (bf16[4,48,768]{2,1,0:T(8,128)(2,1)}, bf16[4,48,768]{2,1,0:T(8,128)(2,1)S(1)}, u32[]{:S(2)}, u32[]{:S(2)}) collective-permute-start(bf16[4,48,768]{2,1,0:T(8,128)(2,1)} %dynamic-slice_bitcast_fusion.7), channel_id=1, source_target_pairs={{0,4},{1,5},{2,6},{3,7},{4,0},{5,1},{6,2},{7,3},{8,12},{9,13},{10,... | collective-permute-start | bytes 884744 | tf_op jit(solution)/shard_map/ppermute | solution.py:259
  342.9 39.5 %collective-permute-start.20 = (bf16[4,96,768]{2,1,0:T(8,128)(2,1)}, bf16[4,96,768]{2,1,0:T(8,128)(2,1)}, u32[]{:S(2)}, u32[]{:S(2)}) collective-permute-start(bf16[4,96,768]{2,1,0:T(8,128)(2,1)} %dynamic-slice_bitcast_fusion.5), channel_id=1, source_target_pairs={{0,2},{1,3},{2,0},{3,1},{4,6},{5,7},{6,4},{7,5},{8,10},{9,11},{10,... | collective-permute-start | bytes 1769480 | tf_op jit(solution)/shard_map/ppermute | solution.py:259
  347.8 42.2 %collective-permute-start.14 = (bf16[4,112,768]{2,1,0:T(8,128)(2,1)}, bf16[4,112,768]{2,1,0:T(8,128)(2,1)}, u32[]{:S(2)}, u32[]{:S(2)}) collective-permute-start(bf16[4,112,768]{2,1,0:T(8,128)(2,1)} %dynamic-slice_bitcast_fusion.3), channel_id=1, source_target_pairs={{0,4},{1,5},{2,6},{3,7},{4,0},{5,1},{6,2},{7,3},{8,12},{9,13},{10,... | collective-permute-start | bytes 2064392 | tf_op jit(solution)/shard_map/ppermute | solution.py:259
  383.8 9.7 %collective-permute-start.23 = (bf16[96,768]{1,0:T(8,128)(2,1)S(1)}, bf16[96,768]{1,0:T(8,128)(2,1)S(1)}, u32[]{:S(2)}, u32[]{:S(2)}) collective-permute-start(bf16[96,768]{1,0:T(8,128)(2,1)S(1)} %get-tuple-element.119), channel_id=1, source_target_pairs={{0,24},{1,25},{2,26},{3,27},{4,28},{5,29},{6,30},{7,31},{8,0},{9,1... | collective-permute-start | bytes 442376 | tf_op jit(solution)/shard_map/ppermute | solution.py:259
  387.1 22.6 %collective-permute-start.22 = (bf16[96,768]{1,0:T(8,128)(2,1)S(1)}, bf16[96,768]{1,0:T(8,128)(2,1)S(1)}, u32[]{:S(2)}, u32[]{:S(2)}) collective-permute-start(bf16[96,768]{1,0:T(8,128)(2,1)S(1)} %get-tuple-element.120), channel_id=1, source_target_pairs={{0,16},{1,17},{2,18},{3,19},{4,20},{5,21},{6,22},{7,23},{8,24},{9,... | collective-permute-start | bytes 442376 | tf_op jit(solution)/shard_map/ppermute | solution.py:259
  388.1 21.6 %collective-permute-start.21 = (bf16[96,768]{1,0:T(8,128)(2,1)S(1)}, bf16[96,768]{1,0:T(8,128)(2,1)S(1)}, u32[]{:S(2)}, u32[]{:S(2)}) collective-permute-start(bf16[96,768]{1,0:T(8,128)(2,1)S(1)} %get-tuple-element.118), channel_id=1, source_target_pairs={{0,8},{1,9},{2,10},{3,11},{4,12},{5,13},{6,14},{7,15},{8,16},{9,17... | collective-permute-start | bytes 442376 | tf_op jit(solution)/shard_map/ppermute | solution.py:259
  391.4 19.1 %collective-permute-start.17 = (bf16[112,768]{1,0:T(8,128)(2,1)S(1)}, bf16[112,768]{1,0:T(8,128)(2,1)S(1)}, u32[]{:S(2)}, u32[]{:S(2)}) collective-permute-start(bf16[112,768]{1,0:T(8,128)(2,1)S(1)} %get-tuple-element.116), channel_id=1, source_target_pairs={{0,24},{1,25},{2,26},{3,27},{4,28},{5,29},{6,30},{7,31},{8,0},{9,1... | collective-permute-start | bytes 516104 | tf_op jit(solution)/shard_map/ppermute | solution.py:259
  393.3 21.1 %collective-permute-start.16 = (bf16[112,768]{1,0:T(8,128)(2,1)S(1)}, bf16[112,768]{1,0:T(8,128)(2,1)S(1)}, u32[]{:S(2)}, u32[]{:S(2)}) collective-permute-start(bf16[112,768]{1,0:T(8,128)(2,1)S(1)} %get-tuple-element.117), channel_id=1, source_target_pairs={{0,16},{1,17},{2,18},{3,19},{4,20},{5,21},{6,22},{7,23},{8,24},{9,... | collective-permute-start | bytes 516104 | tf_op jit(solution)/shard_map/ppermute | solution.py:259
  393.5 21.0 %collective-permute-start.15 = (bf16[112,768]{1,0:T(8,128)(2,1)S(1)}, bf16[112,768]{1,0:T(8,128)(2,1)S(1)}, u32[]{:S(2)}, u32[]{:S(2)}) collective-permute-start(bf16[112,768]{1,0:T(8,128)(2,1)S(1)} %get-tuple-element.115), channel_id=1, source_target_pairs={{0,8},{1,9},{2,10},{3,11},{4,12},{5,13},{6,14},{7,15},{8,16},{9,17... | collective-permute-start | bytes 516104 | tf_op jit(solution)/shard_map/ppermute | solution.py:259
  445.1 17.8 %collective-permute-start.24 = (bf16[4,2,2,64,768]{4,3,0,2,1:T(8,128)(2,1)}, bf16[4,2,2,64,768]{4,3,0,2,1:T(8,128)(2,1)}, u32[]{:S(2)}, u32[]{:S(2)}) collective-permute-start(bf16[4,2,2,64,768]{4,3,0,2,1:T(8,128)(2,1)} %bitcast.327), channel_id=1, source_target_pairs={{0,1},{1,0},{2,3},{3,2},{4,5},{5,4},{6,7},{7,6},{8,9},{9,8},{10,11... | collective-permute-start | bytes 4718600 | tf_op jit(solution)/shard_map/ppermute | solution.py:259
  445.8 9.7 %collective-permute-start.34 = (bf16[48,768]{1,0:T(8,128)(2,1)}, bf16[48,768]{1,0:T(8,128)(2,1)}, u32[]{:S(2)}, u32[]{:S(2)}) collective-permute-start(bf16[48,768]{1,0:T(8,128)(2,1)} %get-tuple-element.130), channel_id=1, source_target_pairs={{0,16},{1,17},{2,18},{3,19},{4,20},{5,21},{6,22},{7,23},{8,24},{9,... | collective-permute-start | bytes 221192 | tf_op jit(solution)/shard_map/ppermute | solution.py:259
  447.5 8.0 %collective-permute-start.33 = (bf16[48,768]{1,0:T(8,128)(2,1)}, bf16[48,768]{1,0:T(8,128)(2,1)}, u32[]{:S(2)}, u32[]{:S(2)}) collective-permute-start(bf16[48,768]{1,0:T(8,128)(2,1)} %get-tuple-element.128), channel_id=1, source_target_pairs={{0,8},{1,9},{2,10},{3,11},{4,12},{5,13},{6,14},{7,15},{8,16},{9,17... | collective-permute-start | bytes 221192 | tf_op jit(solution)/shard_map/ppermute | solution.py:259
  465.1 19.4 %collective-permute-start.25 = (bf16[4,2,64,768]{3,2,0,1:T(8,128)(2,1)S(1)}, bf16[4,2,64,768]{3,2,0,1:T(8,128)(2,1)S(1)}, u32[]{:S(2)}, u32[]{:S(2)}) collective-permute-start(bf16[4,2,64,768]{3,2,0,1:T(8,128)(2,1)S(1)} %dynamic-slice_bitcast_fusion.2), channel_id=1, source_target_pairs={{0,4},{1,5},{2,6},{3,7},{4,0},{5,1},{6,2},{7,3},{8,12},{9,13},{10,... | collective-permute-start | bytes 2359304 | tf_op jit(solution)/shard_map/ppermute | solution.py:259
  484.7 10.2 %collective-permute-start.26 = (bf16[4,64,768]{2,1,0:T(8,128)(2,1)S(1)}, bf16[4,64,768]{2,1,0:T(8,128)(2,1)S(1)}, u32[]{:S(2)}, u32[]{:S(2)}) collective-permute-start(bf16[4,64,768]{2,1,0:T(8,128)(2,1)S(1)} %dynamic-slice_bitcast_fusion.6), channel_id=1, source_target_pairs={{0,2},{1,3},{2,0},{3,1},{4,6},{5,7},{6,4},{7,5},{8,10},{9,11},{10,... | collective-permute-start | bytes 1179656 | tf_op jit(solution)/shard_map/ppermute | solution.py:259
  495.5 8.8 %collective-permute-start.28 = (bf16[64,768]{1,0:T(8,128)(2,1)S(1)}, bf16[64,768]{1,0:T(8,128)(2,1)S(1)}, u32[]{:S(2)}, u32[]{:S(2)}) collective-permute-start(bf16[64,768]{1,0:T(8,128)(2,1)S(1)} %get-tuple-element.123), channel_id=1, source_target_pairs={{0,16},{1,17},{2,18},{3,19},{4,20},{5,21},{6,22},{7,23},{8,24},{9,... | collective-permute-start | bytes 294920 | tf_op jit(solution)/shard_map/ppermute | solution.py:259
  (66 other events, 493.5 us)
Sparse Core Ops, SparseCore 0:
  13.0 98.4 all-gather.1
